TPU v7x, 32 devices: a whole 2x2x4 slice. The times are simulated.
32 devices in a mesh: gz: 8 (over z, y), gx: 2 (over x), gy: 2 (over core).
Axes of the slice: x: 2, y: 2, z: 4, core: 2. Of those that a mesh axis runs over, the one named last changes fastest.
Arguments:
- electric: float32 [3, 128, 32, 256], P(None, 'gz', 'gx', 'gy'), may hold values from -6 to 6
- magnetic: float32 [3, 128, 32, 256], P(None, 'gz', 'gx', 'gy'), may hold values from -6 to 6
- aux_state: float32 [4, 2, 8, 32, 256], P(None, None, None, 'gx', 'gy'), may hold values from -6 to 6
- material: int32 [32, 256], P('gx', 'gy'), may hold values 0 or 1
- kerr_strength: float32 [2], replicated, may hold values from 0.1 to 1
Outputs:
- electric_out: float32 [3, 128, 32, 256], P(None, 'gz', 'gx', 'gy')
- magnetic_out: float32 [3, 128, 32, 256], P(None, 'gz', 'gx', 'gy')
Inputs may be any that keep to these rules, and one draw needn't show every extreme that they name: `material`: 0 marks cladding, 1 the waveguide core.
All inputs are finite; a program needn't handle non-finite values. No bound on the sum of `material` on one device may be relied on, other than what follows from the above.
Results may differ from a plain program's by a relative error of at most 0.00002.
Values sent between devices are 32-bit elements; how exact they have to be, the bound alone decides.
A program may use at most 128 MiB of HBM per device.

v0:
```python
import jax
import jax.numpy as jnp
from jax import lax
from jax.sharding import PartitionSpec as P

PML = 8
STEPS = 4


courant = 0.5
pml_rate = 3.0
eps_clad = 2.085
eps_core = 4.0


def from_behind(shard, axis, by):
    length = lax.axis_size(axis)
    pairs = [(i, i + by) for i in range(length) if 0 <= i + by < length]
    return lax.ppermute(shard, axis, pairs)


def shifted(value, axis, steps):
    count = lax.axis_size(axis)
    pairs = [(source, (source + steps) % count) for source in range(count)]
    return lax.ppermute(value, axis, pairs)


def decay_rates(layer):
    depth_front = (layer - jnp.arange(layer)).astype(jnp.float32) / layer
    depth_back = (jnp.arange(layer) + 1).astype(jnp.float32) / layer
    depth = jnp.stack([depth_front, depth_back])
    return jnp.exp(-pml_rate * depth**3)


def forward_z(values, edge):
    return jnp.concatenate([values[1:], edge], 0) - values


def forward_x(values, edge):
    return jnp.concatenate([values[:, 1:], edge], 1) - values


def forward_y(values, edge):
    return jnp.concatenate([values[:, :, 1:], edge[:, :, None]], 2) - values


def backward_z(values, edge):
    return values - jnp.concatenate([edge, values[:-1]], 0)


def backward_x(values, edge):
    return values - jnp.concatenate([edge, values[:, :-1]], 1)


def backward_y(values, edge):
    return values - jnp.concatenate([edge[:, :, None], values[:, :, :-1]], 2)


def edge_layer(active_end, state_old, boundary, depth_rates):

    def renew():
        renewed = (
            depth_rates[:, None, None] * state_old + (depth_rates - 1.0)[:, None, None] * boundary
        )
        return (renewed, boundary + renewed)

    def keep():
        return (state_old, boundary)

    return lax.cond(active_end, renew, keep)


def absorb(derivative, state_pair, rates, at_front, at_back, back_start):
    layer = state_pair.shape[1]
    front_state, leading = edge_layer(at_front, state_pair[0], derivative[:layer], rates[0])
    back_state, trailing = edge_layer(
        at_back, state_pair[1], derivative[back_start : back_start + layer], rates[1]
    )
    merged = jnp.concatenate(
        [leading, derivative[layer:back_start], trailing, derivative[back_start + layer :]], 0
    )
    return (merged, jnp.stack([front_state, back_state]))


def next_planes(electric):
    return from_behind(electric[0:2, 0:1], "gz", -1)


def shards(electric, magnetic, aux_state, material, kerr_strength):
    planes = electric.shape[1]
    position = lax.axis_index("gz")
    at_front = position == 0
    at_back = position == lax.axis_size("gz") - 1
    rates = decay_rates(PML)
    core = material == 1
    eps_lin = jnp.where(core, eps_core, eps_clad).astype(jnp.float32)
    kerr_cell = jnp.where(core, kerr_strength[1], kerr_strength[0])
    aux_list = [aux_state[0], aux_state[1], aux_state[2], aux_state[3]]
    back_start = planes - PML
    e_next = next_planes(electric)
    for step_index in range(STEPS):
        elec_x, elec_y, elec_z = (electric[0], electric[1], electric[2])
        magn_x, magn_y, magn_z = (magnetic[0], magnetic[1], magnetic[2])
        next_cols = shifted(electric[1:3, :, 0:1, :], "gx", -1)
        next_rows = shifted(jnp.stack([elec_x[:, :, 0], elec_z[:, :, 0]]), "gy", -1)
        slope_y, aux_list[0] = absorb(
            forward_z(elec_y, e_next[1]), aux_list[0], rates, at_front, at_back, back_start
        )
        slope_x, aux_list[1] = absorb(
            forward_z(elec_x, e_next[0]), aux_list[1], rates, at_front, at_back, back_start
        )
        magn_x = magn_x - courant * (forward_y(elec_z, next_rows[1]) - slope_y)
        magn_y = magn_y - courant * (slope_x - forward_x(elec_z, next_cols[1]))
        magn_z = magn_z - courant * (
            forward_x(elec_y, next_cols[0]) - forward_y(elec_x, next_rows[0])
        )
        magnetic = jnp.stack([magn_x, magn_y, magn_z])
        h_prev = from_behind(magnetic[0:2, planes - 1 :], "gz", 1)
        prev_cols = shifted(magnetic[1:3, :, -1:, :], "gx", 1)
        prev_rows = shifted(jnp.stack([magn_x[:, :, -1], magn_z[:, :, -1]]), "gy", 1)
        factor = courant / (
            eps_lin + kerr_cell * (elec_x * elec_x + elec_y * elec_y + elec_z * elec_z)
        )
        slope_hy, aux_list[2] = absorb(
            backward_z(magn_y, h_prev[1]), aux_list[2], rates, at_front, at_back, back_start
        )
        slope_hx, aux_list[3] = absorb(
            backward_z(magn_x, h_prev[0]), aux_list[3], rates, at_front, at_back, back_start
        )
        new_x = elec_x + factor * (backward_y(magn_z, prev_rows[1]) - slope_hy)
        new_y = elec_y + factor * (slope_hx - backward_x(magn_z, prev_cols[1]))
        new_z = elec_z + factor * (
            backward_x(magn_y, prev_cols[0]) - backward_y(magn_x, prev_rows[0])
        )
        fields = jnp.stack([new_x, new_y, new_z, magn_x, magn_y, magn_z])
        arrived = from_behind(fields[:, 0:1], "gz", -1)
        fields = jnp.concatenate([fields[:, 1:], arrived], 1)
        if step_index + 1 < STEPS:
            e_next = next_planes(fields[0:3])
        electric = fields[0:3]
        magnetic = fields[3:6]
    return (electric, magnetic)


def solution(mesh):
    in_specs = (
        P(None, "gz", "gx", "gy"),
        P(None, "gz", "gx", "gy"),
        P(None, None, None, "gx", "gy"),
        P("gx", "gy"),
        P(),
    )
    out_specs = (P(None, "gz", "gx", "gy"), P(None, "gz", "gx", "gy"))
    return jax.shard_map(shards, mesh=mesh, in_specs=in_specs, out_specs=out_specs, check_vma=False)
```

profile of v0, /device:TPU:20, one launch (start us, length us, event | category | flops | bytes accessed | tf_op | source)
XLA Modules:
  0.0 139.2 jit_solution(2243149256276021890)
XLA Ops:
  0.6 1.0 slice_bitcast_fusion.19
  2.1 2.4 %collective-permute-start.2 = (f32[2,1,16,128]{3,2,1,0:T(8,128)S(1)}, f32[2,1,16,128]{3,2,1,0:T(8,128)S(1)}, u32[]{:S(2)}, u32[]{:S(2)}) collective-permute-start(f32[2,1,16,128]{3,2,1,0:T(8,128)S(1)} %slice.793), channel_id=1, source_target_pairs={{4,0},{8,4},{12,8},{16,12},{20,16},{24,20},{28,24},{5,1},{9,5},{13... | collective-permute-start | bytes 49160 | tf_op jit(solution)/shard_map/ppermute | solution.py:19
  4.5 1.6 %collective-permute-start = (f32[2,16,1,128]{3,2,1,0:T(1,128)S(1)}, f32[2,16,1,128]{3,2,1,0:T(1,128)S(1)}, u32[]{:S(2)}, u32[]{:S(2)}) collective-permute-start(f32[2,16,1,128]{3,2,1,0:T(1,128)S(1)} %slice.781), channel_id=1, source_target_pairs={{0,2},{2,0},{1,3},{3,1},{4,6},{6,4},{5,7},{7,5},{8,10},{10,8},{9,1... | collective-permute-start | bytes 49160 | tf_op jit(solution)/shard_map/ppermute | solution.py:25
  6.1 0.8 slice_bitcast_fusion.89
  6.9 1.0 copy-done.9
  9.8 1.2 broadcast_select_fusion
  13.5 0.7 slice_bitcast_fusion.14
  14.3 0.7 slice_bitcast_fusion.12
  15.7 0.7 slice.1013
  16.3 4.3 %collective-permute-start.4 = (f32[2,1,16,128]{3,2,1,0:T(8,128)S(1)}, f32[2,1,16,128]{3,2,1,0:T(8,128)S(1)}, u32[]{:S(2)}, u32[]{:S(2)}) collective-permute-start(f32[2,1,16,128]{3,2,1,0:T(8,128)S(1)} %pad_maximum_fusion.14), channel_id=1, source_target_pairs={{0,4},{4,8},{8,12},{12,16},{16,20},{20,24},{24,28},{1,5},{5,9},{9,... | collective-permute-start | bytes 49160 | tf_op jit(solution)/shard_map/ppermute | solution.py:19
  20.8 0.8 copy.547
  22.8 0.7 copy-done.43
  23.5 1.1 constant_dynamic-update-slice_fusion.4
  26.8 1.6 %collective-permute-done.5 = f32[2,16,1,128]{3,2,1,0:T(1,128)S(1)} collective-permute-done((f32[2,16,1,128]{3,2,1,0:T(1,128)S(1)}, f32[2,16,1,128]{3,2,1,0:T(1,128)S(1)}, u32[]{:S(2)}, u32[]{:S(2)}) %collective-permute-start.5) | collective-permute-done | bytes 16416 | tf_op jit(solution)/shard_map/ppermute | solution.py:25
  28.5 4.2 %collective-permute-start.9 = (f32[2,1,16,128]{3,2,1,0:T(8,128)S(1)}, f32[2,1,16,128]{3,2,1,0:T(8,128)S(1)}, u32[]{:S(2)}, u32[]{:S(2)}) collective-permute-start(f32[2,1,16,128]{3,2,1,0:T(8,128)S(1)} %pad_maximum_fusion.12), channel_id=1, source_target_pairs={{4,0},{8,4},{12,8},{16,12},{20,16},{24,20},{28,24},{5,1},{9,5},{13... | collective-permute-start | bytes 49160 | tf_op jit(solution)/shard_map/ppermute | solution.py:19
  33.0 1.9 %collective-permute-start.6 = (f32[6,1,16,128]{3,2,1,0:T(8,128)S(1)}, f32[6,1,16,128]{3,2,1,0:T(8,128)S(1)}, u32[]{:S(2)}, u32[]{:S(2)}) collective-permute-start(f32[6,1,16,128]{3,2,1,0:T(8,128)S(1)} %slice.1023), channel_id=1, source_target_pairs={{4,0},{8,4},{12,8},{16,12},{20,16},{24,20},{28,24},{5,1},{9,5},{13... | collective-permute-start | bytes 147464 | tf_op jit(solution)/shard_map/ppermute | solution.py:19
  35.4 4.4 %collective-permute-done.6 = f32[6,1,16,128]{3,2,1,0:T(8,128)S(1)} collective-permute-done((f32[6,1,16,128]{3,2,1,0:T(8,128)S(1)}, f32[6,1,16,128]{3,2,1,0:T(8,128)S(1)}, u32[]{:S(2)}, u32[]{:S(2)}) %collective-permute-start.6) | collective-permute-done | bytes 49184 | tf_op jit(solution)/shard_map/ppermute | solution.py:19
  42.4 0.8 copy.551
  43.2 2.0 %collective-permute-done.7 = f32[2,16,1,128]{3,1,2,0:T(8,128)} collective-permute-done((f32[2,16,1,128]{3,1,2,0:T(8,128)}, f32[2,16,1,128]{3,1,2,0:T(8,128)}, u32[]{:S(2)}, u32[]{:S(2)}) %collective-permute-start.7) | collective-permute-done | bytes 16416 | tf_op jit(solution)/shard_map/ppermute | solution.py:25
  45.2 0.7 fusion.199
  46.6 0.7 slice_bitcast_fusion.11
  47.4 0.7 slice_bitcast_fusion.10
  50.0 2.0 %collective-permute-start.11 = (f32[2,1,16,128]{3,2,1,0:T(8,128)S(1)}, f32[2,1,16,128]{3,2,1,0:T(8,128)S(1)}, u32[]{:S(2)}, u32[]{:S(2)}) collective-permute-start(f32[2,1,16,128]{3,2,1,0:T(8,128)S(1)} %pad_maximum_fusion.11), channel_id=1, source_target_pairs={{0,4},{4,8},{8,12},{12,16},{16,20},{20,24},{24,28},{1,5},{5,9},{9,... | collective-permute-start | bytes 49160 | tf_op jit(solution)/shard_map/ppermute | solution.py:19
  52.0 0.8 copy.555
  52.8 0.8 copy.558
  53.7 1.9 %collective-permute-done.11 = f32[2,1,16,128]{3,2,1,0:T(8,128)S(1)} collective-permute-done((f32[2,1,16,128]{3,2,1,0:T(8,128)S(1)}, f32[2,1,16,128]{3,2,1,0:T(8,128)S(1)}, u32[]{:S(2)}, u32[]{:S(2)}) %collective-permute-start.11) | collective-permute-done | bytes 16416 | tf_op jit(solution)/shard_map/ppermute | solution.py:19
  57.6 0.7 copy-done.40
  58.2 1.8 %constant_dynamic-update-slice_fusion.9 = (f32[6,16,16,128]{3,2,1,0:T(8,128)S(1)}, f32[1,16,16,128]{3,2,1,0:T(8,128)}, f32[1,16,16,128]{3,2,1,0:T(8,128)S(1)}) fusion(f32[1,16,16,128]{3,2,1,0:T(8,128)S(1)} %get-tuple-element.1325, f32[1,8,16,128]{3,2,1,0:T(8,128)S(1)} %bitcast.411, f32[1,8,16,128]{3,2,1,0:T(8,128)S(1)} %bitcast.406, ...), kind=kLoop, calls=%fused_computation.378 | loop fusion | flops 720895 | bytes 2113536
  62.4 1.5 %collective-permute-done.12 = f32[2,16,1,128]{3,2,1,0:T(1,128)S(1)} collective-permute-done((f32[2,16,1,128]{3,2,1,0:T(1,128)S(1)}, f32[2,16,1,128]{3,2,1,0:T(1,128)S(1)}, u32[]{:S(2)}, u32[]{:S(2)}) %collective-permute-start.12) | collective-permute-done | bytes 16416 | tf_op jit(solution)/shard_map/ppermute | solution.py:25
  64.0 0.8 copy-done.7
  64.8 2.0 %collective-permute-start.16 = (f32[2,1,16,128]{3,2,1,0:T(8,128)S(1)}, f32[2,1,16,128]{3,2,1,0:T(8,128)S(1)}, u32[]{:S(2)}, u32[]{:S(2)}) collective-permute-start(f32[2,1,16,128]{3,2,1,0:T(8,128)S(1)} %pad_maximum_fusion.9), channel_id=1, source_target_pairs={{4,0},{8,4},{12,8},{16,12},{20,16},{24,20},{28,24},{5,1},{9,5},{13... | collective-permute-start | bytes 49160 | tf_op jit(solution)/shard_map/ppermute | solution.py:19
  67.1 3.8 %collective-permute-start.13 = (f32[6,1,16,128]{3,2,1,0:T(8,128)S(1)}, f32[6,1,16,128]{3,2,1,0:T(8,128)S(1)}, u32[]{:S(2)}, u32[]{:S(2)}) collective-permute-start(f32[6,1,16,128]{3,2,1,0:T(8,128)S(1)} %slice.1075), channel_id=1, source_target_pairs={{4,0},{8,4},{12,8},{16,12},{20,16},{24,20},{28,24},{5,1},{9,5},{13... | collective-permute-start | bytes 147464 | tf_op jit(solution)/shard_map/ppermute | solution.py:19
  71.5 2.6 %collective-permute-done.13 = f32[6,1,16,128]{3,2,1,0:T(8,128)S(1)} collective-permute-done((f32[6,1,16,128]{3,2,1,0:T(8,128)S(1)}, f32[6,1,16,128]{3,2,1,0:T(8,128)S(1)}, u32[]{:S(2)}, u32[]{:S(2)}) %collective-permute-start.13) | collective-permute-done | bytes 49184 | tf_op jit(solution)/shard_map/ppermute | solution.py:19
  77.8 0.8 copy.560
  78.6 0.8 collective-permute-done.14
  79.4 1.3 fusion.197
  80.8 0.7 slice_bitcast_fusion.7
  81.7 0.7 slice_bitcast_fusion.6
  83.6 0.7 slice.1117
  84.2 3.9 %collective-permute-start.18 = (f32[2,1,16,128]{3,2,1,0:T(8,128)S(1)}, f32[2,1,16,128]{3,2,1,0:T(8,128)S(1)}, u32[]{:S(2)}, u32[]{:S(2)}) collective-permute-start(f32[2,1,16,128]{3,2,1,0:T(8,128)S(1)} %pad_maximum_fusion.8), channel_id=1, source_target_pairs={{0,4},{4,8},{8,12},{12,16},{16,20},{20,24},{24,28},{1,5},{5,9},{9,... | collective-permute-start | bytes 49160 | tf_op jit(solution)/shard_map/ppermute | solution.py:19
  88.2 0.8 copy.564
  89.0 0.8 copy.567
  91.8 0.7 copy-done.44
  92.5 1.8 %constant_dynamic-update-slice_fusion.14 = (f32[6,16,16,128]{3,2,1,0:T(8,128)S(1)}, f32[1,16,16,128]{3,2,1,0:T(8,128)}, f32[1,16,16,128]{3,2,1,0:T(8,128)S(1)}) fusion(f32[1,16,16,128]{3,2,1,0:T(8,128)S(1)} %get-tuple-element.1321, f32[1,8,16,128]{3,2,1,0:T(8,128)S(1)} %bitcast.413, f32[1,8,16,128]{3,2,1,0:T(8,128)S(1)} %bitcast.408, ...), kind=kLoop, calls=%fused_computation.383 | loop fusion | flops 720895 | bytes 2113536
  94.4 1.0 collective-permute-start.19
  96.7 1.5 %collective-permute-done.19 = f32[2,16,1,128]{3,2,1,0:T(1,128)S(1)} collective-permute-done((f32[2,16,1,128]{3,2,1,0:T(1,128)S(1)}, f32[2,16,1,128]{3,2,1,0:T(1,128)S(1)}, u32[]{:S(2)}, u32[]{:S(2)}) %collective-permute-start.19) | collective-permute-done | bytes 16416 | tf_op jit(solution)/shard_map/ppermute | solution.py:25
  98.3 0.8 copy-done.8
  99.1 3.9 %collective-permute-start.23 = (f32[2,1,16,128]{3,2,1,0:T(8,128)S(1)}, f32[2,1,16,128]{3,2,1,0:T(8,128)S(1)}, u32[]{:S(2)}, u32[]{:S(2)}) collective-permute-start(f32[2,1,16,128]{3,2,1,0:T(8,128)S(1)} %pad_maximum_fusion.6), channel_id=1, source_target_pairs={{4,0},{8,4},{12,8},{16,12},{20,16},{24,20},{28,24},{5,1},{9,5},{13... | collective-permute-start | bytes 49160 | tf_op jit(solution)/shard_map/ppermute | solution.py:19
  103.3 1.9 %collective-permute-start.20 = (f32[6,1,16,128]{3,2,1,0:T(8,128)S(1)}, f32[6,1,16,128]{3,2,1,0:T(8,128)S(1)}, u32[]{:S(2)}, u32[]{:S(2)}) collective-permute-start(f32[6,1,16,128]{3,2,1,0:T(8,128)S(1)} %slice.1127), channel_id=1, source_target_pairs={{4,0},{8,4},{12,8},{16,12},{20,16},{24,20},{28,24},{5,1},{9,5},{13... | collective-permute-start | bytes 147464 | tf_op jit(solution)/shard_map/ppermute | solution.py:19
  105.8 4.4 %collective-permute-done.20 = f32[6,1,16,128]{3,2,1,0:T(8,128)S(1)} collective-permute-done((f32[6,1,16,128]{3,2,1,0:T(8,128)S(1)}, f32[6,1,16,128]{3,2,1,0:T(8,128)S(1)}, u32[]{:S(2)}, u32[]{:S(2)}) %collective-permute-start.20) | collective-permute-done | bytes 49184 | tf_op jit(solution)/shard_map/ppermute | solution.py:19
  110.7 1.0 collective-permute-start.21
  113.8 0.8 copy.571
  115.2 0.7 slice_bitcast_fusion.3
  117.2 0.7 slice.1169
  117.8 2.0 %collective-permute-start.25 = (f32[2,1,16,128]{3,2,1,0:T(8,128)S(1)}, f32[2,1,16,128]{3,2,1,0:T(8,128)S(1)}, u32[]{:S(2)}, u32[]{:S(2)}) collective-permute-start(f32[2,1,16,128]{3,2,1,0:T(8,128)S(1)} %pad_maximum_fusion.5), channel_id=1, source_target_pairs={{0,4},{4,8},{8,12},{12,16},{16,20},{20,24},{24,28},{1,5},{5,9},{9,... | collective-permute-start | bytes 49160 | tf_op jit(solution)/shard_map/ppermute | solution.py:19
  119.9 0.8 copy.575
  120.9 2.6 %collective-permute-done.25 = f32[2,1,16,128]{3,2,1,0:T(8,128)S(1)} collective-permute-done((f32[2,1,16,128]{3,2,1,0:T(8,128)S(1)}, f32[2,1,16,128]{3,2,1,0:T(8,128)S(1)}, u32[]{:S(2)}, u32[]{:S(2)}) %collective-permute-start.25) | collective-permute-done | bytes 16416 | tf_op jit(solution)/shard_map/ppermute | solution.py:19
  125.4 0.7 copy-done.42
  126.1 1.2 fusion.106
  127.3 1.2 collective-permute-start.26
  129.9 1.2 collective-permute-done.26
  131.4 1.9 %collective-permute-start.27 = (f32[6,1,16,128]{3,2,1,0:T(8,128)S(1)}, f32[6,1,16,128]{3,2,1,0:T(8,128)S(1)}, u32[]{:S(2)}, u32[]{:S(2)}) collective-permute-start(f32[6,1,16,128]{3,2,1,0:T(8,128)S(1)} %slice.1179), channel_id=1, source_target_pairs={{4,0},{8,4},{12,8},{16,12},{20,16},{24,20},{28,24},{5,1},{9,5},{13... | collective-permute-start | bytes 147464 | tf_op jit(solution)/shard_map/ppermute | solution.py:19
  133.4 4.9 %collective-permute-done.27 = f32[6,1,16,128]{3,2,1,0:T(8,128)S(1)} collective-permute-done((f32[6,1,16,128]{3,2,1,0:T(8,128)S(1)}, f32[6,1,16,128]{3,2,1,0:T(8,128)S(1)}, u32[]{:S(2)}, u32[]{:S(2)}) %collective-permute-start.27) | collective-permute-done | bytes 49184 | tf_op jit(solution)/shard_map/ppermute | solution.py:19
  138.3 0.9 pad_maximum_fusion
  (379 shorter events, 37.2 us)
Async XLA Ops:
  0.6 1.4 %copy-start = (f32[3,16,16,128]{3,2,1,0:T(8,128)S(1)}, f32[3,16,16,128]{3,2,1,0:T(8,128)}, u32[]{:S(2)}) copy-start(f32[3,16,16,128]{3,2,1,0:T(8,128)} %param.69) | copy-start | bytes 1179652
  2.0 9.1 %collective-permute-start.1 = (f32[2,16,16]{2,1,0:T(8,128)S(1)}, f32[2,16,16]{2,1,0:T(8,128)S(1)}, u32[]{:S(2)}, u32[]{:S(2)}) collective-permute-start(f32[2,16,16]{2,1,0:T(8,128)S(1)} %pad_maximum_fusion.15), channel_id=1, source_target_pairs={{0,1},{1,0},{2,3},{3,2},{4,5},{5,4},{6,7},{7,6},{8,9},{9,8},{10,11... | collective-permute-start | bytes 6152 | tf_op jit(solution)/shard_map/ppermute | solution.py:25
  2.1 9.8 %collective-permute-start.2 = (f32[2,1,16,128]{3,2,1,0:T(8,128)S(1)}, f32[2,1,16,128]{3,2,1,0:T(8,128)S(1)}, u32[]{:S(2)}, u32[]{:S(2)}) collective-permute-start(f32[2,1,16,128]{3,2,1,0:T(8,128)S(1)} %slice.793), channel_id=1, source_target_pairs={{4,0},{8,4},{12,8},{16,12},{20,16},{24,20},{28,24},{5,1},{9,5},{13... | collective-permute-start | bytes 49160 | tf_op jit(solution)/shard_map/ppermute | solution.py:19
  4.5 7.5 %collective-permute-start = (f32[2,16,1,128]{3,2,1,0:T(1,128)S(1)}, f32[2,16,1,128]{3,2,1,0:T(1,128)S(1)}, u32[]{:S(2)}, u32[]{:S(2)}) collective-permute-start(f32[2,16,1,128]{3,2,1,0:T(1,128)S(1)} %slice.781), channel_id=1, source_target_pairs={{0,2},{2,0},{1,3},{3,1},{4,6},{6,4},{5,7},{7,5},{8,10},{10,8},{9,1... | collective-permute-start | bytes 49160 | tf_op jit(solution)/shard_map/ppermute | solution.py:25
  6.8 1.0 copy-start.9
  7.9 0.7 copy-start.49
  11.1 11.6 %copy-start.29 = (f32[1,8]{1,0:T(1,128)}, f32[1,8]{1,0:T(1,128)S(1)}, u32[]{:S(2)}) copy-start(f32[1,8]{1,0:T(1,128)S(1)} %get-tuple-element.1474) | copy-start | bytes 100
  11.1 11.6 %copy-start.61 = (f32[8]{0:T(128)}, f32[8]{0:T(128)S(1)}, u32[]{:S(2)}) copy-start(f32[8]{0:T(128)S(1)} %get-tuple-element.1473) | copy-start | bytes 100
  11.1 11.7 %copy-start.19 = (f32[1,8]{1,0:T(1,128)}, f32[1,8]{1,0:T(1,128)S(1)}, u32[]{:S(2)}) copy-start(f32[1,8]{1,0:T(1,128)S(1)} %get-tuple-element.1475) | copy-start | bytes 100
  11.1 11.7 %copy-start.51 = (f32[8]{0:T(128)}, f32[8]{0:T(128)S(1)}, u32[]{:S(2)}) copy-start(f32[8]{0:T(128)S(1)} %get-tuple-element.1472) | copy-start | bytes 100
  11.9 1.0 copy-start.1
  15.0 5.7 %collective-permute-start.3 = (f32[2,16,16]{2,1,0:T(8,128)S(1)}, f32[2,16,16]{2,1,0:T(8,128)S(1)}, u32[]{:S(2)}, u32[]{:S(2)}) collective-permute-start(f32[2,16,16]{2,1,0:T(8,128)S(1)} %pad_maximum_fusion.16), channel_id=1, source_target_pairs={{0,1},{1,0},{2,3},{3,2},{4,5},{5,4},{6,7},{7,6},{8,9},{9,8},{10,11... | collective-permute-start | bytes 6152 | tf_op jit(solution)/shard_map/ppermute | solution.py:25
  16.3 5.7 %collective-permute-start.4 = (f32[2,1,16,128]{3,2,1,0:T(8,128)S(1)}, f32[2,1,16,128]{3,2,1,0:T(8,128)S(1)}, u32[]{:S(2)}, u32[]{:S(2)}) collective-permute-start(f32[2,1,16,128]{3,2,1,0:T(8,128)S(1)} %pad_maximum_fusion.14), channel_id=1, source_target_pairs={{0,4},{4,8},{8,12},{12,16},{16,20},{20,24},{24,28},{1,5},{5,9},{9,... | collective-permute-start | bytes 49160 | tf_op jit(solution)/shard_map/ppermute | solution.py:19
  22.8 0.7 copy-start.43
  24.5 0.9 copy-start.17
  24.5 0.9 copy-start.47
  24.6 3.8 %collective-permute-start.5 = (f32[2,16,1,128]{3,2,1,0:T(1,128)S(1)}, f32[2,16,1,128]{3,2,1,0:T(1,128)S(1)}, u32[]{:S(2)}, u32[]{:S(2)}) collective-permute-start(f32[2,16,1,128]{3,2,1,0:T(1,128)S(1)} %pad_maximum_fusion.13), channel_id=1, source_target_pairs={{0,2},{2,0},{1,3},{3,1},{4,6},{6,4},{5,7},{7,5},{8,10},{10,8},{9,1... | collective-permute-start | bytes 49160 | tf_op jit(solution)/shard_map/ppermute | solution.py:25
  25.5 0.7 copy-start.62
  26.8 1.6 %copy-start.4 = (f32[1,16,15,128]{3,2,1,0:T(8,128)S(1)}, f32[1,16,15,128]{3,2,1,0:T(8,128)}, u32[]{:S(2)}) copy-start(f32[1,16,15,128]{3,2,1,0:T(8,128)} %slice_bitcast_fusion.14) | copy-start | bytes 368644
  28.4 4.3 %copy-start.14 = (f32[1,16,16,1]{3,2,1,0:T(8,128)S(1)}, f32[1,16,16,1]{3,2,1,0:T(8,128)}, u32[]{:S(2)}) copy-start(f32[1,16,16,1]{3,2,1,0:T(8,128)} %copy.547) | copy-start | bytes 3076
  28.4 4.3 %copy-start.12 = (f32[1,16,16,127]{3,2,1,0:T(8,128)S(1)}, f32[1,16,16,127]{3,2,1,0:T(8,128)}, u32[]{:S(2)}) copy-start(f32[1,16,16,127]{3,2,1,0:T(8,128)} %slice_bitcast_fusion.12) | copy-start | bytes 390148
  28.5 4.3 %copy-start.13 = (f32[1,16,15,128]{3,2,1,0:T(8,128)S(1)}, f32[1,16,15,128]{3,2,1,0:T(8,128)}, u32[]{:S(2)}) copy-start(f32[1,16,15,128]{3,2,1,0:T(8,128)} %slice_bitcast_fusion.13) | copy-start | bytes 368644
  28.5 6.9 %collective-permute-start.9 = (f32[2,1,16,128]{3,2,1,0:T(8,128)S(1)}, f32[2,1,16,128]{3,2,1,0:T(8,128)S(1)}, u32[]{:S(2)}, u32[]{:S(2)}) collective-permute-start(f32[2,1,16,128]{3,2,1,0:T(8,128)S(1)} %pad_maximum_fusion.12), channel_id=1, source_target_pairs={{4,0},{8,4},{12,8},{16,12},{20,16},{24,20},{28,24},{5,1},{9,5},{13... | collective-permute-start | bytes 49160 | tf_op jit(solution)/shard_map/ppermute | solution.py:19
  33.0 6.9 %collective-permute-start.6 = (f32[6,1,16,128]{3,2,1,0:T(8,128)S(1)}, f32[6,1,16,128]{3,2,1,0:T(8,128)S(1)}, u32[]{:S(2)}, u32[]{:S(2)}) collective-permute-start(f32[6,1,16,128]{3,2,1,0:T(8,128)S(1)} %slice.1023), channel_id=1, source_target_pairs={{4,0},{8,4},{12,8},{16,12},{20,16},{24,20},{28,24},{5,1},{9,5},{13... | collective-permute-start | bytes 147464 | tf_op jit(solution)/shard_map/ppermute | solution.py:19
  40.5 1.4 collective-permute-start.8
  41.2 4.1 %collective-permute-start.7 = (f32[2,16,1,128]{3,1,2,0:T(8,128)}, f32[2,16,1,128]{3,1,2,0:T(8,128)}, u32[]{:S(2)}, u32[]{:S(2)}) collective-permute-start(f32[2,16,1,128]{3,1,2,0:T(8,128)} %bitcast.211), channel_id=1, source_target_pairs={{0,2},{2,0},{1,3},{3,1},{4,6},{6,4},{5,7},{7,5},{8,10},{10,8},{9,1... | collective-permute-start | bytes 49160 | tf_op jit(solution)/shard_map/ppermute | solution.py:25
  48.4 3.6 %collective-permute-start.10 = (f32[2,16,16]{2,1,0:T(8,128)S(1)}, f32[2,16,16]{2,1,0:T(8,128)S(1)}, u32[]{:S(2)}, u32[]{:S(2)}) collective-permute-start(f32[2,16,16]{2,1,0:T(8,128)S(1)} %pad_maximum_fusion.18), channel_id=1, source_target_pairs={{0,1},{1,0},{2,3},{3,2},{4,5},{5,4},{6,7},{7,6},{8,9},{9,8},{10,11... | collective-permute-start | bytes 6152 | tf_op jit(solution)/shard_map/ppermute | solution.py:25
  50.0 5.6 %collective-permute-start.11 = (f32[2,1,16,128]{3,2,1,0:T(8,128)S(1)}, f32[2,1,16,128]{3,2,1,0:T(8,128)S(1)}, u32[]{:S(2)}, u32[]{:S(2)}) collective-permute-start(f32[2,1,16,128]{3,2,1,0:T(8,128)S(1)} %pad_maximum_fusion.11), channel_id=1, source_target_pairs={{0,4},{4,8},{8,12},{12,16},{16,20},{20,24},{24,28},{1,5},{5,9},{9,... | collective-permute-start | bytes 49160 | tf_op jit(solution)/shard_map/ppermute | solution.py:19
  56.2 0.7 copy-start.63
  57.5 0.7 copy-start.40
  60.1 0.9 copy-start.16
  60.1 0.9 copy-start.46
  60.1 3.8 %collective-permute-start.12 = (f32[2,16,1,128]{3,2,1,0:T(1,128)S(1)}, f32[2,16,1,128]{3,2,1,0:T(1,128)S(1)}, u32[]{:S(2)}, u32[]{:S(2)}) collective-permute-start(f32[2,16,1,128]{3,2,1,0:T(1,128)S(1)} %pad_maximum_fusion.10), channel_id=1, source_target_pairs={{0,2},{2,0},{1,3},{3,1},{4,6},{6,4},{5,7},{7,5},{8,10},{10,8},{9,1... | collective-permute-start | bytes 49160 | tf_op jit(solution)/shard_map/ppermute | solution.py:25
  61.0 0.7 copy-start.64
  62.4 1.6 %copy-start.11 = (f32[1,16,15,128]{3,2,1,0:T(8,128)S(1)}, f32[1,16,15,128]{3,2,1,0:T(8,128)}, u32[]{:S(2)}) copy-start(f32[1,16,15,128]{3,2,1,0:T(8,128)} %slice_bitcast_fusion.10) | copy-start | bytes 368644
  63.9 0.9 copy-start.7
  64.8 2.1 %copy-start.3 = (f32[1,16,15,128]{3,2,1,0:T(8,128)S(1)}, f32[1,16,15,128]{3,2,1,0:T(8,128)}, u32[]{:S(2)}) copy-start(f32[1,16,15,128]{3,2,1,0:T(8,128)} %slice_bitcast_fusion.9) | copy-start | bytes 368644
  64.8 2.1 %copy-start.6 = (f32[1,16,16,1]{3,2,1,0:T(8,128)S(1)}, f32[1,16,16,1]{3,2,1,0:T(8,128)}, u32[]{:S(2)}) copy-start(f32[1,16,16,1]{3,2,1,0:T(8,128)} %copy.558) | copy-start | bytes 3076
  64.8 6.7 %collective-permute-start.16 = (f32[2,1,16,128]{3,2,1,0:T(8,128)S(1)}, f32[2,1,16,128]{3,2,1,0:T(8,128)S(1)}, u32[]{:S(2)}, u32[]{:S(2)}) collective-permute-start(f32[2,1,16,128]{3,2,1,0:T(8,128)S(1)} %pad_maximum_fusion.9), channel_id=1, source_target_pairs={{4,0},{8,4},{12,8},{16,12},{20,16},{24,20},{28,24},{5,1},{9,5},{13... | collective-permute-start | bytes 49160 | tf_op jit(solution)/shard_map/ppermute | solution.py:19
  67.1 6.9 %collective-permute-start.13 = (f32[6,1,16,128]{3,2,1,0:T(8,128)S(1)}, f32[6,1,16,128]{3,2,1,0:T(8,128)S(1)}, u32[]{:S(2)}, u32[]{:S(2)}) collective-permute-start(f32[6,1,16,128]{3,2,1,0:T(8,128)S(1)} %slice.1075), channel_id=1, source_target_pairs={{4,0},{8,4},{12,8},{16,12},{20,16},{24,20},{28,24},{5,1},{9,5},{13... | collective-permute-start | bytes 147464 | tf_op jit(solution)/shard_map/ppermute | solution.py:19
  74.6 2.7 %collective-permute-start.15 = (f32[2,16,16]{2,1,0:T(8,128)S(1)}, f32[2,16,16]{2,1,0:T(8,128)S(1)}, u32[]{:S(2)}, u32[]{:S(2)}) collective-permute-start(f32[2,16,16]{2,1,0:T(8,128)S(1)} %pad_maximum_fusion.19), channel_id=1, source_target_pairs={{0,1},{1,0},{2,3},{3,2},{4,5},{5,4},{6,7},{7,6},{8,9},{9,8},{10,11... | collective-permute-start | bytes 6152 | tf_op jit(solution)/shard_map/ppermute | solution.py:25
  75.3 4.1 %collective-permute-start.14 = (f32[2,16,1,128]{3,2,1,0:T(1,128)}, f32[2,16,1,128]{3,2,1,0:T(1,128)}, u32[]{:S(2)}, u32[]{:S(2)}) collective-permute-start(f32[2,16,1,128]{3,2,1,0:T(1,128)} %fusion.131), channel_id=1, source_target_pairs={{0,2},{2,0},{1,3},{3,1},{4,6},{6,4},{5,7},{7,5},{8,10},{10,8},{9,1... | collective-permute-start | bytes 49160 | tf_op jit(solution)/shard_map/ppermute | solution.py:25
  76.0 0.7 copy-start.65
  82.7 5.5 %collective-permute-start.17 = (f32[2,16,16]{2,1,0:T(8,128)S(1)}, f32[2,16,16]{2,1,0:T(8,128)S(1)}, u32[]{:S(2)}, u32[]{:S(2)}) collective-permute-start(f32[2,16,16]{2,1,0:T(8,128)S(1)} %pad_maximum_fusion.20), channel_id=1, source_target_pairs={{0,1},{1,0},{2,3},{3,2},{4,5},{5,4},{6,7},{7,6},{8,9},{9,8},{10,11... | collective-permute-start | bytes 6152 | tf_op jit(solution)/shard_map/ppermute | solution.py:25
  84.2 5.6 %collective-permute-start.18 = (f32[2,1,16,128]{3,2,1,0:T(8,128)S(1)}, f32[2,1,16,128]{3,2,1,0:T(8,128)S(1)}, u32[]{:S(2)}, u32[]{:S(2)}) collective-permute-start(f32[2,1,16,128]{3,2,1,0:T(8,128)S(1)} %pad_maximum_fusion.8), channel_id=1, source_target_pairs={{0,4},{4,8},{8,12},{12,16},{16,20},{20,24},{24,28},{1,5},{5,9},{9,... | collective-permute-start | bytes 49160 | tf_op jit(solution)/shard_map/ppermute | solution.py:19
  91.8 0.7 copy-start.44
  94.4 1.0 copy-start.15
  94.4 1.0 copy-start.45
  94.4 3.8 %collective-permute-start.19 = (f32[2,16,1,128]{3,2,1,0:T(1,128)S(1)}, f32[2,16,1,128]{3,2,1,0:T(1,128)S(1)}, u32[]{:S(2)}, u32[]{:S(2)}) collective-permute-start(f32[2,16,1,128]{3,2,1,0:T(1,128)S(1)} %pad_maximum_fusion.7), channel_id=1, source_target_pairs={{0,2},{2,0},{1,3},{3,1},{4,6},{6,4},{5,7},{7,5},{8,10},{10,8},{9,1... | collective-permute-start | bytes 49160 | tf_op jit(solution)/shard_map/ppermute | solution.py:25
  96.7 1.5 %copy-start.10 = (f32[1,16,15,128]{3,2,1,0:T(8,128)S(1)}, f32[1,16,15,128]{3,2,1,0:T(8,128)}, u32[]{:S(2)}) copy-start(f32[1,16,15,128]{3,2,1,0:T(8,128)} %slice_bitcast_fusion.6) | copy-start | bytes 368644
  98.2 0.9 copy-start.8
  99.1 3.9 %copy-start.2 = (f32[1,16,15,128]{3,2,1,0:T(8,128)S(1)}, f32[1,16,15,128]{3,2,1,0:T(8,128)}, u32[]{:S(2)}) copy-start(f32[1,16,15,128]{3,2,1,0:T(8,128)} %slice_bitcast_fusion.5) | copy-start | bytes 368644
  99.1 4.0 %copy-start.5 = (f32[1,16,16,1]{3,2,1,0:T(8,128)S(1)}, f32[1,16,16,1]{3,2,1,0:T(8,128)}, u32[]{:S(2)}) copy-start(f32[1,16,16,1]{3,2,1,0:T(8,128)} %copy.567) | copy-start | bytes 3076
  99.1 6.7 %collective-permute-start.23 = (f32[2,1,16,128]{3,2,1,0:T(8,128)S(1)}, f32[2,1,16,128]{3,2,1,0:T(8,128)S(1)}, u32[]{:S(2)}, u32[]{:S(2)}) collective-permute-start(f32[2,1,16,128]{3,2,1,0:T(8,128)S(1)} %pad_maximum_fusion.6), channel_id=1, source_target_pairs={{4,0},{8,4},{12,8},{16,12},{20,16},{24,20},{28,24},{5,1},{9,5},{13... | collective-permute-start | bytes 49160 | tf_op jit(solution)/shard_map/ppermute | solution.py:19
  103.3 6.9 %collective-permute-start.20 = (f32[6,1,16,128]{3,2,1,0:T(8,128)S(1)}, f32[6,1,16,128]{3,2,1,0:T(8,128)S(1)}, u32[]{:S(2)}, u32[]{:S(2)}) collective-permute-start(f32[6,1,16,128]{3,2,1,0:T(8,128)S(1)} %slice.1127), channel_id=1, source_target_pairs={{4,0},{8,4},{12,8},{16,12},{20,16},{24,20},{28,24},{5,1},{9,5},{13... | collective-permute-start | bytes 147464 | tf_op jit(solution)/shard_map/ppermute | solution.py:19
  110.7 4.0 %collective-permute-start.21 = (f32[2,16,1,128]{3,1,2,0:T(8,128)S(1)}, f32[2,16,1,128]{3,1,2,0:T(8,128)S(1)}, u32[]{:S(2)}, u32[]{:S(2)}) collective-permute-start(f32[2,16,1,128]{3,1,2,0:T(8,128)S(1)} %bitcast.472), channel_id=1, source_target_pairs={{0,2},{2,0},{1,3},{3,1},{4,6},{6,4},{5,7},{7,5},{8,10},{10,8},{9,1... | collective-permute-start | bytes 49160 | tf_op jit(solution)/shard_map/ppermute | solution.py:25
  111.8 1.5 %collective-permute-start.22 = (f32[2,16,16]{2,1,0:T(8,128)S(1)}, f32[2,16,16]{2,1,0:T(8,128)S(1)}, u32[]{:S(2)}, u32[]{:S(2)}) collective-permute-start(f32[2,16,16]{2,1,0:T(8,128)S(1)} %pad_maximum_fusion.21), channel_id=1, source_target_pairs={{0,1},{1,0},{2,3},{3,2},{4,5},{5,4},{6,7},{7,6},{8,9},{9,8},{10,11... | collective-permute-start | bytes 6152 | tf_op jit(solution)/shard_map/ppermute | solution.py:25
  116.4 3.4 %collective-permute-start.24 = (f32[2,16,16]{2,1,0:T(8,128)S(1)}, f32[2,16,16]{2,1,0:T(8,128)S(1)}, u32[]{:S(2)}, u32[]{:S(2)}) collective-permute-start(f32[2,16,16]{2,1,0:T(8,128)S(1)} %pad_maximum_fusion.22), channel_id=1, source_target_pairs={{0,1},{1,0},{2,3},{3,2},{4,5},{5,4},{6,7},{7,6},{8,9},{9,8},{10,11... | collective-permute-start | bytes 6152 | tf_op jit(solution)/shard_map/ppermute | solution.py:25
  117.8 5.6 %collective-permute-start.25 = (f32[2,1,16,128]{3,2,1,0:T(8,128)S(1)}, f32[2,1,16,128]{3,2,1,0:T(8,128)S(1)}, u32[]{:S(2)}, u32[]{:S(2)}) collective-permute-start(f32[2,1,16,128]{3,2,1,0:T(8,128)S(1)} %pad_maximum_fusion.5), channel_id=1, source_target_pairs={{0,4},{4,8},{8,12},{12,16},{16,20},{20,24},{24,28},{1,5},{5,9},{9,... | collective-permute-start | bytes 49160 | tf_op jit(solution)/shard_map/ppermute | solution.py:19
  125.4 0.7 copy-start.42
  127.3 1.2 copy-start.18
  127.3 1.2 copy-start.48
  127.3 3.8 %collective-permute-start.26 = (f32[2,16,1,128]{3,2,1,0:T(1,128)S(1)}, f32[2,16,1,128]{3,2,1,0:T(1,128)S(1)}, u32[]{:S(2)}, u32[]{:S(2)}) collective-permute-start(f32[2,16,1,128]{3,2,1,0:T(1,128)S(1)} %pad_maximum_fusion.4), channel_id=1, source_target_pairs={{0,2},{2,0},{1,3},{3,1},{4,6},{6,4},{5,7},{7,5},{8,10},{10,8},{9,1... | collective-permute-start | bytes 49160 | tf_op jit(solution)/shard_map/ppermute | solution.py:25
  131.4 6.9 %collective-permute-start.27 = (f32[6,1,16,128]{3,2,1,0:T(8,128)S(1)}, f32[6,1,16,128]{3,2,1,0:T(8,128)S(1)}, u32[]{:S(2)}, u32[]{:S(2)}) collective-permute-start(f32[6,1,16,128]{3,2,1,0:T(8,128)S(1)} %slice.1179), channel_id=1, source_target_pairs={{4,0},{8,4},{12,8},{16,12},{20,16},{24,20},{28,24},{5,1},{9,5},{13... | collective-permute-start | bytes 147464 | tf_op jit(solution)/shard_map/ppermute | solution.py:19
  (35 other events, 21.9 us)
where the time goes:
time: 141 us; the launch traced here: 139 us
  local copies, waits for them, and re-layouts  51.1 us (36%)
  starting transfers between devices  42.5 us (30%)
  waiting for transfers between devices  31.4 us (22%)
  other arithmetic  11.8 us (8%)
  between operations  2.28 us (2%)
    ppermute x12, starting transfers between devices, from_behind(): return lax.ppermute(shard, axis, pairs)  34.4 us
    ppermute x12, waiting for transfers between devices, from_behind(): return lax.ppermute(shard, axis, pairs)  22.8 us
    unnamed x154, local copies, waits for them, and re-layouts  21.1 us
    ppermute x16, waiting for transfers between devices, shifted(): return lax.ppermute(value, axis, pairs)  8.59 us
    ppermute x16, starting transfers between devices, shifted(): return lax.ppermute(value, axis, pairs)  8.04 us
    concatenate x20, local copies, waits for them, and re-layouts, backward_y(): return values - jnp.concatenate([edge[:, :, None], values[:, :, :-1]], 2)  7.99 us
    unnamed x12, other arithmetic  6.64 us
    concatenate x17, local copies, waits for them, and re-layouts, forward_y(): return jnp.concatenate([values[:, :, 1:], edge[:, :, None]], 2) - values  4.49 us
  transfers between devices with their start and end apart: 28, of which 16 were waited for; matrix products, arithmetic and copies ran while one was open for 14% of the time, Pallas kernels for 0%

commit v1 on v0

v1 whole, which is shorter than its diff:
```python
import functools

import jax
import jax.numpy as jnp
import numpy as np
from jax import lax
from jax.experimental import pallas as pl
from jax.experimental.pallas import tpu as pltpu
from jax.sharding import PartitionSpec as P

PML = 8
STEPS = 4
HALO = 2 * STEPS
COLS = STEPS

courant = 0.5
pml_rate = 3.0
eps_clad = 2.085
eps_core = 4.0

MESH = pl.DeviceIdType.MESH
DEPTH_RATES = [
    float(np.exp(np.float32(-pml_rate) * np.float32((m + 1) / PML) ** 3)) for m in range(PML)
]


def kernel(
    sizes,
    kerr_ref, elec, magn, aux, material,
    elec_out, magn_out,
    F, A, eps_ref, kap_ref, mat,
    pack, pack_aux, pack_mat,
    halo, halo_aux, halo_mat,
    local_sem, send_sem, recv_sem,
):
    n_gz, n_gx, n_gy = sizes
    planes, cols, rows = elec.shape[1:]
    wide = cols + 2 * COLS
    pairs = planes // 2
    first = HALO // 2
    gz, gx, gy = lax.axis_index("gz"), lax.axis_index("gx"), lax.axis_index("gy")
    has_pred, has_succ = gz > 0, gz < n_gz - 1
    at_front, at_back = gz == 0, gz == n_gz - 1
    at_edge = jnp.logical_or(at_front, at_back)
    left = {"gx": lax.rem(gx + n_gx - 1, n_gx)}
    right = {"gx": lax.rem(gx + 1, n_gx)}
    other = {"gy": lax.rem(gy + 1, n_gy)}
    pred = {"gz": jnp.maximum(gz - 1, 0)}
    succ = {"gz": jnp.minimum(gz + 1, n_gz - 1)}
    own, far = pl.ds(0, rows), pl.ds(rows, rows)

    side = jnp.where(at_front, 0, 1)
    loads = [
        pltpu.make_async_copy(elec, F.at[pl.ds(0, 3), pl.ds(0, planes), pl.ds(0, cols), own], local_sem.at[0]),
        pltpu.make_async_copy(magn, F.at[pl.ds(3, 3), pl.ds(0, planes), pl.ds(0, cols), own], local_sem.at[1]),
    ]
    load_aux = pltpu.make_async_copy(
        aux.at[:, side], A.at[:, :, pl.ds(0, cols), own], local_sem.at[2]
    )
    for load in loads:
        load.start()

    @pl.when(at_edge)
    def _():
        load_aux.start()

    barrier = pltpu.get_barrier_semaphore()
    for peer in (left, right, other):
        pl.semaphore_signal(barrier, inc=1, device_id=peer, device_id_type=MESH)

    @pl.when(has_pred)
    def _():
        pl.semaphore_signal(barrier, inc=1, device_id=pred, device_id_type=MESH)

    @pl.when(has_succ)
    def _():
        pl.semaphore_signal(barrier, inc=1, device_id=succ, device_id_type=MESH)

    pl.semaphore_wait(barrier, 3 + has_pred.astype(jnp.int32) + has_succ.astype(jnp.int32))

    count = [0]

    def remote(src, dst, peer):
        at = count[0]
        count[0] += 1
        return pltpu.make_async_remote_copy(
            src_ref=src, dst_ref=dst, send_sem=send_sem.at[at], recv_sem=recv_sem.at[at],
            device_id=peer, device_id_type=MESH,
        )

    def fields(lo, n, at, width, lanes):
        return F.at[pl.ds(lo, 3), pl.ds(at, n), pl.ds(0, width), lanes]

    x_first = [remote(pack.at[d, pl.ds(0, first)], halo.at[d, pl.ds(0, first), :, :, own], p) for d, p in ((0, left), (1, right))]
    x_mat = [remote(pack_mat.at[d], halo_mat.at[d, :, own], p) for d, p in ((0, left), (1, right))]
    x_aux = [remote(pack_aux.at[d], halo_aux.at[d, :, :, :, own], p) for d, p in ((0, left), (1, right))]
    x_rest = [
        remote(pack.at[d, pl.ds(first, pairs - first)], halo.at[d, pl.ds(first, pairs - first), :, :, own], p)
        for d, p in ((0, left), (1, right))
    ]
    z_own = [
        remote(src.at[:, pl.ds(0, HALO)], fields(lo, HALO, planes, cols, own), pred)
        for lo, src in ((0, elec), (3, magn))
    ]
    z_far = [
        remote(halo.at[d, pl.ds(0, first), :, :, own], halo.at[d, pl.ds(pairs, first), :, :, own], pred)
        for d in (0, 1)
    ]
    y_own = [remote(src, fields(lo, planes, 0, cols, far), other) for lo, src in ((0, elec), (3, magn))]
    y_x = [
        remote(halo.at[d, pl.ds(0, pairs), :, :, own], halo.at[d, pl.ds(0, pairs), :, :, far], other)
        for d in (0, 1)
    ]
    y_xz = [
        remote(halo.at[d, pl.ds(pairs, first), :, :, own], halo.at[d, pl.ds(pairs, first), :, :, far], other)
        for d in (0, 1)
    ]
    y_z = [
        remote(fields(lo, HALO, planes, cols, own), fields(lo, HALO, planes, cols, far), other)
        for lo in (0, 3)
    ]
    y_aux = remote(aux.at[:, side], A.at[:, :, pl.ds(0, cols), far], other)
    y_haux = [remote(halo_aux.at[d, :, :, :, own], halo_aux.at[d, :, :, :, far], other) for d in (0, 1)]
    y_hmat = [remote(halo_mat.at[d, :, own], halo_mat.at[d, :, far], other) for d in (0, 1)]
    y_m = remote(mat.at[pl.ds(0, cols), own], mat.at[pl.ds(0, cols), far], other)

    @pl.when(has_pred)
    def _():
        for copy in z_own:
            copy.start()

    for load in loads:
        load.wait()

    def pack_pair(q, _):
        for c in range(6):
            pack[0, q, c, 0:COLS] = F[c, 2 * q, 0:COLS, 0:rows]
            pack[0, q, c, COLS:] = F[c, 2 * q + 1, 0:COLS, 0:rows]
            pack[1, q, c, 0:COLS] = F[c, 2 * q + 1, cols - COLS : cols, 0:rows]
            pack[1, q, c, COLS:] = F[c, 2 * q, cols - COLS : cols, 0:rows]
        return _

    lax.fori_loop(0, first, pack_pair, 0)
    for copy in x_first:
        copy.start()
    m = (material[...] == 1).astype(jnp.float32)
    mat[0:cols, 0:rows] = m
    pack_mat[0] = m[0 : 2 * COLS]
    pack_mat[1] = m[cols - 2 * COLS : cols]
    for copy in x_mat:
        copy.start()
    y_m.start()

    @pl.when(at_edge)
    def _():
        load_aux.wait()

        def pack_aux_pair(q, _):
            for c in range(4):
                pack_aux[0, q, c, 0:COLS] = A[c, 2 * q, 0:COLS, 0:rows]
                pack_aux[0, q, c, COLS:] = A[c, 2 * q + 1, 0:COLS, 0:rows]
                pack_aux[1, q, c, 0:COLS] = A[c, 2 * q + 1, cols - COLS : cols, 0:rows]
                pack_aux[1, q, c, COLS:] = A[c, 2 * q, cols - COLS : cols, 0:rows]
            return _

        lax.fori_loop(0, PML // 2, pack_aux_pair, 0)
        for copy in x_aux:
            copy.start()
        y_aux.start()

    lax.fori_loop(first, pairs, pack_pair, 0)
    for copy in x_rest:
        copy.start()
    for copy in y_own:
        copy.start()

    for copy in x_first:
        copy.wait()

    @pl.when(has_pred)
    def _():
        for copy in z_far:
            copy.start()

    for copy, on in zip(x_mat, y_hmat):
        copy.wait()
        on.start()
    for copy, on in zip(x_rest, y_x):
        copy.wait()
        on.start()

    @pl.when(at_edge)
    def _():
        for copy, on in zip(x_aux, y_haux):
            copy.wait()
            on.start()

    def unpack(q, _):
        low = lax.broadcasted_iota(jnp.int32, (2 * COLS, 2 * rows), 0) < COLS
        for c in range(6):
            r, l = halo[0, q, c], halo[1, q, c]
            F[c, 2 * q, cols:wide] = jnp.where(low, r, l)
            F[c, 2 * q + 1, cols:wide] = pltpu.roll(jnp.where(low, l, r), COLS, 0)
        return _

    def unpack_aux(q, _):
        low = lax.broadcasted_iota(jnp.int32, (2 * COLS, 2 * rows), 0) < COLS
        for c in range(4):
            r, l = halo_aux[0, q, c], halo_aux[1, q, c]
            A[c, 2 * q, cols:wide] = jnp.where(low, r, l)
            A[c, 2 * q + 1, cols:wide] = pltpu.roll(jnp.where(low, l, r), COLS, 0)
        return _

    def sweep(s, lo, hi):
        shift = s + jnp.where(at_front, 0, planes - PML)

        def plane(a, absorbing):
            ex, ey, ez = F[0, a], F[1, a], F[2, a]
            gy_, gx_ = F[1, a + 1] - ey, F[0, a + 1] - ex
            if absorbing:
                k = a - shift
                m = jnp.where(at_front, PML - 1 - k, k)
                b = jnp.float32(DEPTH_RATES[0])
                for i in range(1, PML):
                    b = jnp.where(m == i, jnp.float32(DEPTH_RATES[i]), b)

                def absorb(c, g):
                    s_new = b * A[c, k] + (b - 1.0) * g
                    A[c, k] = s_new
                    return g + s_new

                gy_, gx_ = absorb(0, gy_), absorb(1, gx_)
            nx, ny = wide - 1, 2 * rows - 1
            hx = F[3, a] - courant * ((pltpu.roll(ez, ny, 1) - ez) - gy_)
            hy = F[4, a] - courant * (gx_ - (pltpu.roll(ez, nx, 0) - ez))
            hz = F[5, a] - courant * ((pltpu.roll(ey, nx, 0) - ey) - (pltpu.roll(ex, ny, 1) - ex))
            F[3, a], F[4, a], F[5, a] = hx, hy, hz
            factor = courant / (eps_ref[...] + kap_ref[...] * (ex * ex + ey * ey + ez * ez))
            before = jnp.maximum(a - 1, 0)
            hy_, hx_ = hy - F[4, before], hx - F[3, before]
            if absorbing:
                hy_, hx_ = absorb(2, hy_), absorb(3, hx_)
            F[0, a] = ex + factor * ((hz - pltpu.roll(hz, 1, 1)) - hy_)
            F[1, a] = ey + factor * (hx_ - (hz - pltpu.roll(hz, 1, 0)))
            F[2, a] = ez + factor * ((hy - pltpu.roll(hy, 1, 0)) - (hx - pltpu.roll(hx, 1, 1)))

        def body(a, _):
            inside = jnp.logical_and(at_edge, jnp.logical_and(a >= shift, a < shift + PML))

            @pl.when(inside)
            def _():
                plane(a, True)

            @pl.when(jnp.logical_not(inside))
            def _():
                plane(a, False)

            return _

        lax.fori_loop(lo, hi, body, None)

    for copy in y_hmat + y_x + y_own + [y_m]:
        copy.wait()

    @pl.when(at_edge)
    def _():
        for copy in y_haux + [y_aux]:
            copy.wait()
        lax.fori_loop(0, PML // 2, unpack_aux, 0)

    lax.fori_loop(0, pairs, unpack, 0)
    low = lax.broadcasted_iota(jnp.int32, (2 * COLS, 2 * rows), 0) < COLS
    mat[cols:wide] = jnp.where(low, halo_mat[0], halo_mat[1])
    core = mat[...] > 0.5
    eps_ref[...] = jnp.where(core, jnp.float32(eps_core), jnp.float32(eps_clad))
    kap_ref[...] = jnp.where(core, kerr_ref[1], kerr_ref[0])

    def early(s, _):
        sweep(s, s, planes - 1 - s)
        return _

    @pl.when(has_succ)
    def _():
        for copy in z_own + z_far:
            copy.wait_recv()
        for copy in y_z + y_xz:
            copy.start()

    lax.fori_loop(0, STEPS, early, 0)

    @pl.when(has_pred)
    def _():
        for copy in z_own + z_far:
            copy.wait_send()

    @pl.when(has_succ)
    def _():
        for copy in y_z + y_xz:
            copy.wait()
        lax.fori_loop(pairs, pairs + first, unpack, 0)

    @pl.when(at_back)
    def _():
        def clear(a, _):
            for c in range(6):
                F[c, a] = jnp.zeros((wide, 2 * rows), jnp.float32)
            return _

        lax.fori_loop(planes, planes + HALO, clear, 0)

    def late(s, _):
        hi = jnp.where(at_back, jnp.minimum(planes + s, planes + HALO - 1 - s), planes + HALO - 1 - s)
        sweep(s, planes - 1 - s, hi)
        return _

    lax.fori_loop(0, STEPS, late, 0)

    stores = [
        pltpu.make_async_copy(fields(lo, planes, STEPS, cols, own), out, local_sem.at[at])
        for at, (lo, out) in enumerate(((0, elec_out), (3, magn_out)))
    ]
    for store in stores:
        store.start()
    for store in stores:
        store.wait()


def shards(sizes, electric, magnetic, aux_state, material, kerr_strength):
    _, planes, cols, rows = electric.shape
    wide, deep = cols + 2 * COLS, planes + HALO
    f32 = jnp.float32
    any_space = pl.BlockSpec(memory_space=pl.ANY)
    vmem = pl.BlockSpec(memory_space=pltpu.VMEM)
    shape = jax.ShapeDtypeStruct(electric.shape, f32)
    return pl.pallas_call(
        functools.partial(kernel, sizes),
        out_shape=(shape, shape),
        in_specs=[pl.BlockSpec(memory_space=pltpu.SMEM), any_space, any_space, any_space, vmem],
        out_specs=(any_space, any_space),
        scratch_shapes=[
            pltpu.VMEM((6, deep, wide, 2 * rows), f32),
            pltpu.VMEM((4, PML, wide, 2 * rows), f32),
            pltpu.VMEM((wide, 2 * rows), f32),
            pltpu.VMEM((wide, 2 * rows), f32),
            pltpu.VMEM((wide, 2 * rows), f32),
            pltpu.VMEM((2, planes // 2, 6, 2 * COLS, rows), f32),
            pltpu.VMEM((2, PML // 2, 4, 2 * COLS, rows), f32),
            pltpu.VMEM((2, 2 * COLS, rows), f32),
            pltpu.VMEM((2, deep // 2, 6, 2 * COLS, 2 * rows), f32),
            pltpu.VMEM((2, PML // 2, 4, 2 * COLS, 2 * rows), f32),
            pltpu.VMEM((2, 2 * COLS, 2 * rows), f32),
            pltpu.SemaphoreType.DMA((3,)),
            pltpu.SemaphoreType.DMA((32,)),
            pltpu.SemaphoreType.DMA((32,)),
        ],
        compiler_params=pltpu.CompilerParams(
            collective_id=0, has_side_effects=True, vmem_limit_bytes=40 * 2**20
        ),
    )(kerr_strength, electric, magnetic, aux_state, material)


def solution(mesh):
    sizes = tuple(mesh.shape[axis] for axis in ("gz", "gx", "gy"))
    in_specs = (
        P(None, "gz", "gx", "gy"),
        P(None, "gz", "gx", "gy"),
        P(None, None, None, "gx", "gy"),
        P("gx", "gy"),
        P(),
    )
    out_specs = (P(None, "gz", "gx", "gy"), P(None, "gz", "gx", "gy"))
    return jax.shard_map(
        functools.partial(shards, sizes),
        mesh=mesh, in_specs=in_specs, out_specs=out_specs, check_vma=False,
    )
```

time: 141 us -> 40.1 us (0.28)
  the two profiles are of different devices: /device:TPU:20 before, /device:TPU:0 now
where the time goes in v1:
time: 40.1 us; the launch traced here: 39.8 us
  Pallas kernels  33.3 us (83%)
  local copies, waits for them, and re-layouts  5.87 us (15%)
  between operations  0.65 us (2%)
    pallas_call x1, Pallas kernels, shards(): pl.pallas_call(functools.partial(kernel, sizes), out_shape=(shape, shape)...  33.3 us
    unnamed x12, local copies, waits for them, and re-layouts  5.87 us

profile of v1, /device:TPU:0, one launch (start us, length us, event | category | flops | bytes accessed | tf_op | source)
XLA Modules:
  0.0 39.8 jit_solution(8625958528791188546)
XLA Ops:
  0.6 0.0 copy-start
  0.6 1.0 %copy-done = f32[4,2,8,16,128]{4,3,2,1,0:T(8,128)S(1)} copy-done((f32[4,2,8,16,128]{4,3,2,1,0:T(8,128)S(1)}, f32[4,2,8,16,128]{4,3,2,1,0:T(8,128)}, u32[]{:S(2)}) %copy-start) | copy-done | bytes 524312
  1.7 0.0 copy-start.1
  1.7 1.0 %copy-done.1 = f32[3,16,16,128]{3,2,1,0:T(8,128)S(1)} copy-done((f32[3,16,16,128]{3,2,1,0:T(8,128)S(1)}, f32[3,16,16,128]{3,2,1,0:T(8,128)}, u32[]{:S(2)}) %copy-start.1) | copy-done | bytes 393240
  2.7 0.0 copy-start.2
  2.7 1.0 %copy-done.2 = f32[3,16,16,128]{3,2,1,0:T(8,128)S(1)} copy-done((f32[3,16,16,128]{3,2,1,0:T(8,128)S(1)}, f32[3,16,16,128]{3,2,1,0:T(8,128)}, u32[]{:S(2)}) %copy-start.2) | copy-done | bytes 393240
  3.7 0.0 copy-start.3
  3.7 0.7 %copy-done.3 = s32[16,128]{1,0:T(8,128)S(1)} copy-done((s32[16,128]{1,0:T(8,128)S(1)}, s32[16,128]{1,0:T(8,128)}, u32[]{:S(2)}) %copy-start.3) | copy-done | bytes 8216
  4.4 0.0 copy-start.4
  4.4 0.7 %copy-done.4 = f32[2]{0:T(128)S(1)} copy-done((f32[2]{0:T(128)S(1)}, f32[2]{0:T(128)}, u32[]{:S(2)}) %copy-start.4) | copy-done | bytes 32
  5.0 33.3 %shard_map.68 = (f32[3,16,16,128]{3,2,1,0:T(8,128)S(1)}, f32[3,16,16,128]{3,2,1,0:T(8,128)S(1)}) custom-call(f32[2]{0:T(128)S(1)} %copy-done.4, f32[3,16,16,128]{3,2,1,0:T(8,128)S(1)} %copy-done.1, f32[3,16,16,128]{3,2,1,0:T(8,128)S(1)} %copy-done.2, f32[4,2,8,16,128]{4,3,2,1,0:T(8,128)S(1)} %copy-done, s32[16,128]{1,0:T(8,128)S(1)} %copy-done.3), custom_call_target="tpu_custom_call" | custom-call | tf_op jit(solution)/shard_map/pallas_call | solution.py:335
  38.3 0.7 %copy.9 = f32[3,16,16,128]{3,2,1,0:T(8,128)} copy(f32[3,16,16,128]{3,2,1,0:T(8,128)S(1)} %get-tuple-element.4) | data formatting | bytes 786432
  39.1 0.7 %copy.10 = f32[3,16,16,128]{3,2,1,0:T(8,128)} copy(f32[3,16,16,128]{3,2,1,0:T(8,128)S(1)} %get-tuple-element.5) | data formatting | bytes 786432
Async XLA Ops:
  0.6 1.0 %copy-start = (f32[4,2,8,16,128]{4,3,2,1,0:T(8,128)S(1)}, f32[4,2,8,16,128]{4,3,2,1,0:T(8,128)}, u32[]{:S(2)}) copy-start(f32[4,2,8,16,128]{4,3,2,1,0:T(8,128)} %aux.1) | copy-start | bytes 1572868
  1.7 1.0 %copy-start.1 = (f32[3,16,16,128]{3,2,1,0:T(8,128)S(1)}, f32[3,16,16,128]{3,2,1,0:T(8,128)}, u32[]{:S(2)}) copy-start(f32[3,16,16,128]{3,2,1,0:T(8,128)} %elec.1) | copy-start | bytes 1179652
  2.7 1.0 %copy-start.2 = (f32[3,16,16,128]{3,2,1,0:T(8,128)S(1)}, f32[3,16,16,128]{3,2,1,0:T(8,128)}, u32[]{:S(2)}) copy-start(f32[3,16,16,128]{3,2,1,0:T(8,128)} %magn.1) | copy-start | bytes 1179652
  3.7 0.7 %copy-start.3 = (s32[16,128]{1,0:T(8,128)S(1)}, s32[16,128]{1,0:T(8,128)}, u32[]{:S(2)}) copy-start(s32[16,128]{1,0:T(8,128)} %material.1) | copy-start | bytes 24580
  4.4 0.7 %copy-start.4 = (f32[2]{0:T(128)S(1)}, f32[2]{0:T(128)}, u32[]{:S(2)}) copy-start(f32[2]{0:T(128)} %kerr_ref.1) | copy-start | bytes 28

commit v2 on v0

v2 whole, which is shorter than its diff:
```python
import functools

import jax
import jax.numpy as jnp
import numpy as np
from jax import lax
from jax.experimental import pallas as pl
from jax.experimental.pallas import tpu as pltpu
from jax.sharding import PartitionSpec as P

PML = 8
STEPS = 4
HALO = 2 * STEPS
COLS = STEPS
PAD = 4
GROUP = 4

courant = 0.5
pml_rate = 3.0
eps_clad = 2.085
eps_core = 4.0

MESH = pl.DeviceIdType.MESH
DEPTH_RATES = [
    float(np.exp(np.float32(-pml_rate) * np.float32((m + 1) / PML) ** 3)) for m in range(PML)
]


def kernel(
    sizes,
    kerr_ref, elec, magn, aux, material,
    elec_out, magn_out,
    F, A, eps_ref, kap_ref, mat, mat_own, own_fields,
    pack, pack_aux, pack_mat,
    halo, halo_aux, halo_mat,
    local_sem, send_sem, recv_sem, z_send_sem, z_recv_sem,
):
    n_gz, n_gx, n_gy = sizes
    planes, cols, rows = elec.shape[1:]
    wide = cols + 2 * COLS
    half = planes // 2
    quads = half // 2
    pairs = planes // 2
    gz, gx, gy = lax.axis_index("gz"), lax.axis_index("gx"), lax.axis_index("gy")
    low_part, high_part = gy == 0, gy == 1
    has_pred = gz > 0
    takes_z = jnp.logical_and(high_part, gz < n_gz - 1)
    at_front, at_back = gz == 0, gz == n_gz - 1
    at_edge = jnp.logical_or(at_front, at_back)
    left = {"gx": lax.rem(gx + n_gx - 1, n_gx)}
    right = {"gx": lax.rem(gx + 1, n_gx)}
    other = {"gy": 1 - gy}
    pred = {"gz": jnp.maximum(gz - 1, 0), "gy": 1}
    succ = [{"gz": jnp.minimum(gz + 1, n_gz - 1), "gy": part} for part in (0, 1)]
    own, far = pl.ds(0, rows), pl.ds(rows, rows)
    z_lanes = pl.ds(pl.multiple_of((1 - gy) * rows, rows), rows)
    start = half * gy
    side = jnp.where(at_front, 0, 1)
    args = ((0, elec), (3, magn))

    def fields(lo, at, n, width, lanes):
        return F.at[pl.ds(lo, 3), pl.ds(PAD + at, n), pl.ds(0, width), lanes]

    def when(condition, work):
        pl.when(condition)(work)

    def each(copies, method):
        def work():
            for copy in copies:
                getattr(copy, method)()

        return work

    count = [0]

    def local(src, dst):
        count[0] += 1
        return pltpu.make_async_copy(src, dst, local_sem.at[count[0] - 1])

    stage_low = [local(r.at[:, pl.ds(0, half)], own_fields.at[pl.ds(lo, 3), pl.ds(0, half)]) for lo, r in args]
    stage_high = [local(r.at[:, pl.ds(half, half)], own_fields.at[pl.ds(lo, 3), pl.ds(half, half)]) for lo, r in args]
    load_mat = local(material, mat_own)
    load_aux = local(aux.at[:, side], A.at[:, pl.ds(0, PML), pl.ds(0, cols), own])
    load_low = [local(r.at[:, pl.ds(0, half)], fields(lo, 0, half, cols, own)) for lo, r in args]
    load_high = [local(r.at[:, pl.ds(half, half)], fields(lo, half - start, half, cols, own)) for lo, r in args]
    for copy in stage_low + stage_high + [load_mat]:
        copy.start()
    when(at_edge, each([load_aux], "start"))
    when(low_part, each(load_low, "start"))
    each(load_high, "start")()

    barrier = pltpu.get_barrier_semaphore()

    def greet(peers):
        def work():
            for peer in peers:
                pl.semaphore_signal(barrier, inc=1, device_id=peer, device_id_type=MESH)

        return work

    greet([left, right, other])()
    when(has_pred, greet([pred]))
    when(takes_z, greet(succ))
    pl.semaphore_wait(barrier, 3 + has_pred.astype(jnp.int32) + 2 * takes_z.astype(jnp.int32))

    numbered = [0]

    def remote(src, dst, peer):
        at = numbered[0]
        numbered[0] += 1
        return pltpu.make_async_remote_copy(
            src_ref=src, dst_ref=dst, send_sem=send_sem.at[at], recv_sem=recv_sem.at[at],
            device_id=peer, device_id_type=MESH,
        )

    z_numbered = [0]

    def z_remote(src, dst, sender):
        at = z_numbered[0]
        z_numbered[0] += 1
        return pltpu.make_async_remote_copy(
            src_ref=src, dst_ref=dst, send_sem=z_send_sem.at[at], recv_sem=z_recv_sem.at[at, sender],
            device_id=pred, device_id_type=MESH,
        )

    def tiles(d, at, n, lanes):
        return halo.at[d, pl.ds(at, n), :, :, lanes]

    both = ((0, left), (1, right))
    x_low = [remote(pack.at[d, pl.ds(0, quads)], tiles(d, 0, quads, own), p) for d, p in both]
    x_high = [remote(pack.at[d, pl.ds(quads, quads)], tiles(d, quads, quads, own), p) for d, p in both]
    x_mat = [remote(pack_mat.at[d], halo_mat.at[d, :, own], p) for d, p in both]
    x_aux = [remote(pack_aux.at[d], halo_aux.at[d, :, :, :, own], p) for d, p in both]
    y_low = [remote(r.at[:, pl.ds(0, half)], fields(lo, 0, half, cols, far), other) for lo, r in args]
    y_high = [remote(r.at[:, pl.ds(half, half)], fields(lo, start, half, cols, far), other) for lo, r in args]
    yx_low = [remote(tiles(d, 0, quads, own), tiles(d, 0, quads, far), other) for d in (0, 1)]
    yx_high = [remote(tiles(d, quads, quads, own), tiles(d, quads, quads, far), other) for d in (0, 1)]
    y_aux = [remote(aux.at[:, side], A.at[:, pl.ds(0, PML), pl.ds(0, cols), far], other)]
    yx_aux = [remote(halo_aux.at[d, :, :, :, own], halo_aux.at[d, :, :, :, far], other) for d in (0, 1)]
    y_mat = [remote(mat.at[pl.ds(0, cols), own], mat.at[pl.ds(0, cols), far], other)]
    yx_mat = [remote(halo_mat.at[d, :, own], halo_mat.at[d, :, far], other) for d in (0, 1)]

    def z_copies(sender, lanes):
        z_numbered[0] = 0
        sent = [z_remote(r.at[:, pl.ds(0, half)], fields(lo, half, half, cols, lanes), sender) for lo, r in args]
        passed = [z_remote(tiles(d, 0, quads, own), tiles(d, pairs, quads, lanes), sender) for d in (0, 1)]
        return sent, passed

    z_own, z_passed = z_copies(gy, z_lanes)
    z_from = [copy for sender, lanes in ((0, far), (1, own)) for part in z_copies(sender, lanes) for copy in part]

    when(has_pred, each(z_own, "start"))

    def pack_pair(q, carry):
        for c in range(6):
            pack[0, q, c, 0:COLS] = own_fields[c, 2 * q, 0:COLS]
            pack[0, q, c, COLS:] = own_fields[c, 2 * q + 1, 0:COLS]
            pack[1, q, c, 0:COLS] = own_fields[c, 2 * q + 1, cols - COLS : cols]
            pack[1, q, c, COLS:] = own_fields[c, 2 * q, cols - COLS : cols]
        return carry

    each(stage_low, "wait")()
    lax.fori_loop(0, quads, pack_pair, 0)
    each(x_low, "start")()
    each(stage_high, "wait")()
    lax.fori_loop(quads, pairs, pack_pair, 0)
    each(x_high, "start")()
    load_mat.wait()
    m = (mat_own[...] == 1).astype(jnp.float32)
    mat[0:cols, 0:rows] = m
    pack_mat[0] = m[0 : 2 * COLS]
    pack_mat[1] = m[cols - 2 * COLS : cols]
    each(x_mat + y_mat, "start")()

    @pl.when(at_edge)
    def _():
        load_aux.wait()

        def pack_aux_pair(q, carry):
            for c in range(4):
                pack_aux[0, q, c, 0:COLS] = A[c, 2 * q, 0:COLS, 0:rows]
                pack_aux[0, q, c, COLS:] = A[c, 2 * q + 1, 0:COLS, 0:rows]
                pack_aux[1, q, c, 0:COLS] = A[c, 2 * q + 1, cols - COLS : cols, 0:rows]
                pack_aux[1, q, c, COLS:] = A[c, 2 * q, cols - COLS : cols, 0:rows]
            return carry

        lax.fori_loop(0, PML // 2, pack_aux_pair, 0)
        each(x_aux + y_aux, "start")()

    when(high_part, each(y_low, "start"))
    each(y_high, "start")()

    def clear(lo, n):
        def plane(a, carry):
            for c in range(6):
                F[c, a] = jnp.zeros((wide, 2 * rows), jnp.float32)
            return carry

        lax.fori_loop(lo, lo + n, plane, 0)

    clear(0, PAD)
    when(jnp.logical_and(at_back, high_part), lambda: clear(PAD + half, half))

    each(x_low, "wait")()
    when(has_pred, each(z_passed, "start"))
    when(high_part, each(yx_low, "start"))
    each(x_mat, "wait")()
    each(yx_mat, "start")()

    @pl.when(at_edge)
    def _():
        each(x_aux, "wait")()
        each(yx_aux, "start")()

    each(x_high, "wait")()
    each(yx_high, "start")()

    def joined(r, l):
        low = lax.broadcasted_iota(jnp.int32, (2 * COLS, 2 * rows), 0) < COLS
        return jnp.where(low, r, l), pltpu.roll(jnp.where(low, l, r), COLS, 0)

    def unpack(q, carry):
        at = PAD + 2 * q - start
        for c in range(6):
            F[c, at, cols:wide], F[c, at + 1, cols:wide] = joined(halo[0, q, c], halo[1, q, c])
        return carry

    def unpack_aux(q, carry):
        for c in range(4):
            A[c, 2 * q, cols:wide], A[c, 2 * q + 1, cols:wide] = joined(halo_aux[0, q, c], halo_aux[1, q, c])
        return carry

    nx, ny = wide - 1, 2 * rows - 1

    def group(a, s, shift, absorbing):
        E = [[F[c, a + i] for c in range(3)] for i in range(GROUP + 1)]
        H = [[F[c, a + i] for c in range(3, 6)] for i in range(GROUP)]
        before = F[3, a - 1], F[4, a - 1]
        rates = []
        states = []
        if absorbing:
            for i in range(GROUP):
                k = a + i - shift
                inside = jnp.logical_and(k >= 0, k < PML)
                at = jnp.where(inside, k, PML)
                m = jnp.where(at_front, PML - 1 - k, k)
                b = jnp.float32(DEPTH_RATES[0])
                for j in range(1, PML):
                    b = jnp.where(m == j, jnp.float32(DEPTH_RATES[j]), b)
                rates.append((inside, at, b))
                states.append([A[c, at] for c in range(4)])

        new_states = []

        def absorb(c, i, g):
            if not absorbing:
                return g
            inside, at, b = rates[i]
            s_new = b * states[i][c] + (b - 1.0) * g
            new_states.append((c, at, s_new))
            return jnp.where(inside, g + s_new, g)

        new_h = []
        for i in range(GROUP):
            ex, ey, ez = E[i]
            slope_y = absorb(0, i, E[i + 1][1] - ey)
            slope_x = absorb(1, i, E[i + 1][0] - ex)
            hx = H[i][0] - courant * ((pltpu.roll(ez, ny, 1) - ez) - slope_y)
            hy = H[i][1] - courant * (slope_x - (pltpu.roll(ez, nx, 0) - ez))
            hz = H[i][2] - courant * ((pltpu.roll(ey, nx, 0) - ey) - (pltpu.roll(ex, ny, 1) - ex))
            new_h.append((hx, hy, hz))
        new_e = []
        for i in range(GROUP):
            ex, ey, ez = E[i]
            hx, hy, hz = new_h[i]
            below = before if i == 0 else new_h[i - 1]
            factor = courant / (eps_ref[...] + kap_ref[...] * (ex * ex + ey * ey + ez * ez))
            slope_hy = absorb(2, i, hy - below[1])
            slope_hx = absorb(3, i, hx - below[0])
            new_e.append((
                ex + factor * ((hz - pltpu.roll(hz, 1, 1)) - slope_hy),
                ey + factor * (slope_hx - (hz - pltpu.roll(hz, 1, 0))),
                ez + factor * ((hy - pltpu.roll(hy, 1, 0)) - (hx - pltpu.roll(hx, 1, 1))),
            ))
        for i in range(GROUP):
            for c in range(3):
                F[c, a + i] = new_e[i][c]
                F[3 + c, a + i] = new_h[i][c]
        for c, at, value in new_states:
            A[c, at] = value

    def sweep(s, lo, n_groups, top):
        shift = PAD + s + jnp.where(at_front, 0, planes - PML) - start

        def body(g, carry):
            a = PAD + lo + GROUP * g
            inside = jnp.logical_and(at_edge, jnp.logical_and(a + GROUP > shift, a < shift + PML))
            when(inside, lambda: group(a, s, shift, True))
            when(jnp.logical_not(inside), lambda: group(a, s, shift, False))

            if top is not None:
                @pl.when(jnp.logical_and(at_back, high_part))
                def _():
                    def plane(p, carry):
                        for c in range(3):
                            F[c, p] = jnp.zeros((wide, 2 * rows), jnp.float32)
                        return carry

                    lax.fori_loop(jnp.maximum(a, PAD + top), a + GROUP, plane, 0)

            return carry

        lax.fori_loop(0, n_groups, body, 0)

    each(load_high, "wait")()

    @pl.when(low_part)
    def _():
        each(load_low, "wait")()
        each(y_low + yx_low, "wait_recv")()

    when(high_part, each(y_high + yx_high, "wait_recv"))
    each(y_mat + yx_mat, "wait")()

    @pl.when(at_edge)
    def _():
        each(y_aux + yx_aux, "wait")()
        lax.fori_loop(0, PML // 2, unpack_aux, 0)

    lax.fori_loop(quads * gy, quads * gy + quads, unpack, 0)
    low = lax.broadcasted_iota(jnp.int32, (2 * COLS, 2 * rows), 0) < COLS
    mat[cols:wide] = jnp.where(low, halo_mat[0], halo_mat[1])
    core = mat[...] > 0.5
    eps_ref[...] = jnp.where(core, jnp.float32(eps_core), jnp.float32(eps_clad))
    kap_ref[...] = jnp.where(core, kerr_ref[1], kerr_ref[0])

    def early(s, carry):
        n_groups = (half - 1 - 2 * s + GROUP - 1) // GROUP
        sweep(s, half - 1 - s - GROUP * n_groups, n_groups, None)
        return carry

    lax.fori_loop(0, STEPS, early, 0)

    when(low_part, each(y_high + yx_high, "wait_recv"))
    when(takes_z, each(z_from, "wait_recv"))

    @pl.when(jnp.logical_or(low_part, takes_z))
    def _():
        lax.fori_loop(quads * gy + quads, quads * gy + 2 * quads, unpack, 0)

    def late(s, carry):
        sweep(s, half - 1 - s, half // GROUP, half + s)
        return carry

    lax.fori_loop(0, STEPS, late, 0)

    results = ((0, elec_out), (3, magn_out))
    store = [local(fields(lo, STEPS, half, cols, own), r.at[:, pl.ds(start, half)]) for lo, r in results]
    hand = [remote(fields(lo, STEPS, half, cols, far), r.at[:, pl.ds(start, half)], other) for lo, r in results]
    each(hand + store, "start")()
    when(has_pred, each(z_own + z_passed, "wait_send"))
    when(high_part, each(y_low + yx_low, "wait_send"))
    each(y_high + yx_high, "wait_send")()
    each(hand + store, "wait")()


def shards(sizes, electric, magnetic, aux_state, material, kerr_strength):
    _, planes, cols, rows = electric.shape
    wide, deep = cols + 2 * COLS, planes + HALO
    f32 = jnp.float32
    any_space = pl.BlockSpec(memory_space=pl.ANY)
    shape = jax.ShapeDtypeStruct(electric.shape, f32)
    return pl.pallas_call(
        functools.partial(kernel, sizes),
        out_shape=(shape, shape),
        in_specs=[pl.BlockSpec(memory_space=pltpu.SMEM), any_space, any_space, any_space, any_space],
        out_specs=(any_space, any_space),
        scratch_shapes=[
            pltpu.VMEM((6, PAD + planes, wide, 2 * rows), f32),
            pltpu.VMEM((4, PML + 1, wide, 2 * rows), f32),
            pltpu.VMEM((wide, 2 * rows), f32),
            pltpu.VMEM((wide, 2 * rows), f32),
            pltpu.VMEM((wide, 2 * rows), f32),
            pltpu.VMEM((cols, rows), jnp.int32),
            pltpu.VMEM((6, planes, cols, rows), f32),
            pltpu.VMEM((2, planes // 2, 6, 2 * COLS, rows), f32),
            pltpu.VMEM((2, PML // 2, 4, 2 * COLS, rows), f32),
            pltpu.VMEM((2, 2 * COLS, rows), f32),
            pltpu.VMEM((2, deep // 2, 6, 2 * COLS, 2 * rows), f32),
            pltpu.VMEM((2, PML // 2, 4, 2 * COLS, 2 * rows), f32),
            pltpu.VMEM((2, 2 * COLS, 2 * rows), f32),
            pltpu.SemaphoreType.DMA((12,)),
            pltpu.SemaphoreType.DMA((24,)),
            pltpu.SemaphoreType.DMA((24,)),
            pltpu.SemaphoreType.DMA((4,)),
            pltpu.SemaphoreType.DMA((4, 2)),
        ],
        compiler_params=pltpu.CompilerParams(
            collective_id=0, has_side_effects=True, vmem_limit_bytes=60 * 2**20
        ),
    )(kerr_strength, electric, magnetic, aux_state, material)


def solution(mesh):
    sizes = tuple(mesh.shape[axis] for axis in ("gz", "gx", "gy"))
    in_specs = (
        P(None, "gz", "gx", "gy"),
        P(None, "gz", "gx", "gy"),
        P(None, None, None, "gx", "gy"),
        P("gx", "gy"),
        P(),
    )
    out_specs = (P(None, "gz", "gx", "gy"), P(None, "gz", "gx", "gy"))
    return jax.shard_map(
        functools.partial(shards, sizes),
        mesh=mesh, in_specs=in_specs, out_specs=out_specs, check_vma=False,
    )
```

time: 141 us -> 28.8 us (0.20)
  the two profiles are of different devices: /device:TPU:20 before, /device:TPU:0 now
where the time goes in v2:
time: 28.8 us; the launch traced here: 28.6 us
  Pallas kernels  25.4 us (88%)
  local copies, waits for them, and re-layouts  2.57 us (9%)
  between operations  0.65 us (2%)
    pallas_call x1, Pallas kernels, shards(): pl.pallas_call(functools.partial(kernel, sizes), out_shape=(shape, shape)...  25.4 us
    unnamed x4, local copies, waits for them, and re-layouts  2.57 us

profile of v2, /device:TPU:0, one launch (start us, length us, event | category | flops | bytes accessed | tf_op | source)
XLA Modules:
  0.0 28.6 jit_solution(4156210671731637710)
XLA Ops:
  0.6 25.4 %shard_map.68 = (f32[3,16,16,128]{3,2,1,0:T(8,128)}, f32[3,16,16,128]{3,2,1,0:T(8,128)}) custom-call(f32[2]{0:T(128)} %kerr_ref.1, f32[3,16,16,128]{3,2,1,0:T(8,128)} %elec.1, f32[3,16,16,128]{3,2,1,0:T(8,128)} %magn.1, f32[4,2,8,16,128]{4,3,2,1,0:T(8,128)} %aux.1, s32[16,128]{1,0:T(8,128)} %material.1), custom_call_target="tpu_custom_call" | custom-call | tf_op jit(solution)/shard_map/pallas_call | solution.py:373
  26.0 0.0 copy-start
  26.0 1.8 %copy.9 = f32[3,16,16,128]{3,2,1,0:T(8,128)} copy(f32[3,16,16,128]{3,2,1,0:T(8,128)} %get-tuple-element.4) | data formatting | bytes 786432
  27.9 0.0 copy-done
  27.9 0.7 %copy.10 = f32[3,16,16,128]{3,2,1,0:T(8,128)} copy(f32[3,16,16,128]{3,2,1,0:T(8,128)S(1)} %copy-done) | data formatting | bytes 786432
Async XLA Ops:
  26.0 1.8 %copy-start = (f32[3,16,16,128]{3,2,1,0:T(8,128)S(1)}, f32[3,16,16,128]{3,2,1,0:T(8,128)}, u32[]{:S(2)}) copy-start(f32[3,16,16,128]{3,2,1,0:T(8,128)} %get-tuple-element.5) | copy-start | bytes 1179652

commit v3 on v2

--- a/solution.py
+++ b/solution.py
@@ -13,7 +13,8 @@
 HALO = 2 * STEPS
 COLS = STEPS
 PAD = 4
-GROUP = 4
+GROUP = SPAN = 4
+PAIRS = SPAN // 2
 
 courant = 0.5
 pml_rate = 3.0
@@ -127,14 +128,13 @@
         return halo.at[d, pl.ds(at, n), :, :, lanes]
 
     both = ((0, left), (1, right))
-    x_low = [remote(pack.at[d, pl.ds(0, quads)], tiles(d, 0, quads, own), p) for d, p in both]
-    x_high = [remote(pack.at[d, pl.ds(quads, quads)], tiles(d, quads, quads, own), p) for d, p in both]
+    chunks = [(k * PAIRS, PAIRS) for k in range(pairs // PAIRS)]
+    x_halo = [[remote(pack.at[d, pl.ds(at, n)], tiles(d, at, n, own), p) for d, p in both] for at, n in chunks]
     x_mat = [remote(pack_mat.at[d], halo_mat.at[d, :, own], p) for d, p in both]
     x_aux = [remote(pack_aux.at[d], halo_aux.at[d, :, :, :, own], p) for d, p in both]
     y_low = [remote(r.at[:, pl.ds(0, half)], fields(lo, 0, half, cols, far), other) for lo, r in args]
     y_high = [remote(r.at[:, pl.ds(half, half)], fields(lo, start, half, cols, far), other) for lo, r in args]
-    yx_low = [remote(tiles(d, 0, quads, own), tiles(d, 0, quads, far), other) for d in (0, 1)]
-    yx_high = [remote(tiles(d, quads, quads, own), tiles(d, quads, quads, far), other) for d in (0, 1)]
+    yx = [[remote(tiles(d, at, n, own), tiles(d, at, n, far), other) for d in (0, 1)] for at, n in chunks]
     y_aux = [remote(aux.at[:, side], A.at[:, pl.ds(0, PML), pl.ds(0, cols), far], other)]
     yx_aux = [remote(halo_aux.at[d, :, :, :, own], halo_aux.at[d, :, :, :, far], other) for d in (0, 1)]
     y_mat = [remote(mat.at[pl.ds(0, cols), own], mat.at[pl.ds(0, cols), far], other)]
@@ -142,14 +142,20 @@
 
     def z_copies(sender, lanes):
         z_numbered[0] = 0
-        sent = [z_remote(r.at[:, pl.ds(0, half)], fields(lo, half, half, cols, lanes), sender) for lo, r in args]
-        passed = [z_remote(tiles(d, 0, quads, own), tiles(d, pairs, quads, lanes), sender) for d in (0, 1)]
+        sent, passed = [], []
+        for k in range(half // SPAN):
+            sent.append([
+                z_remote(r.at[:, pl.ds(k * SPAN, SPAN)], fields(lo, half + k * SPAN, SPAN, cols, lanes), sender)
+                for lo, r in args
+            ])
+            at, n = chunks[k]
+            passed.append([z_remote(tiles(d, at, n, own), tiles(d, pairs + at, n, lanes), sender) for d in (0, 1)])
         return sent, passed
 
     z_own, z_passed = z_copies(gy, z_lanes)
-    z_from = [copy for sender, lanes in ((0, far), (1, own)) for part in z_copies(sender, lanes) for copy in part]
-
-    when(has_pred, each(z_own, "start"))
+    z_from = [z_copies(0, far), z_copies(1, own)]
+
+    when(has_pred, each(z_own[0], "start"))
 
     def pack_pair(q, carry):
         for c in range(6):
@@ -159,36 +165,37 @@
             pack[1, q, c, COLS:] = own_fields[c, 2 * q, cols - COLS : cols]
         return carry
 
-    each(stage_low, "wait")()
-    lax.fori_loop(0, quads, pack_pair, 0)
-    each(x_low, "start")()
-    each(stage_high, "wait")()
-    lax.fori_loop(quads, pairs, pack_pair, 0)
-    each(x_high, "start")()
+    def pack_aux_pair(q, carry):
+        for c in range(4):
+            pack_aux[0, q, c, 0:COLS] = A[c, 2 * q, 0:COLS, 0:rows]
+            pack_aux[0, q, c, COLS:] = A[c, 2 * q + 1, 0:COLS, 0:rows]
+            pack_aux[1, q, c, 0:COLS] = A[c, 2 * q + 1, cols - COLS : cols, 0:rows]
+            pack_aux[1, q, c, COLS:] = A[c, 2 * q, cols - COLS : cols, 0:rows]
+        return carry
+
+    def send_aux():
+        load_aux.wait()
+        lax.fori_loop(0, PML // 2, pack_aux_pair, 0)
+        each(x_aux + y_aux, "start")()
+
     load_mat.wait()
     m = (mat_own[...] == 1).astype(jnp.float32)
     mat[0:cols, 0:rows] = m
     pack_mat[0] = m[0 : 2 * COLS]
     pack_mat[1] = m[cols - 2 * COLS : cols]
     each(x_mat + y_mat, "start")()
-
-    @pl.when(at_edge)
-    def _():
-        load_aux.wait()
-
-        def pack_aux_pair(q, carry):
-            for c in range(4):
-                pack_aux[0, q, c, 0:COLS] = A[c, 2 * q, 0:COLS, 0:rows]
-                pack_aux[0, q, c, COLS:] = A[c, 2 * q + 1, 0:COLS, 0:rows]
-                pack_aux[1, q, c, 0:COLS] = A[c, 2 * q + 1, cols - COLS : cols, 0:rows]
-                pack_aux[1, q, c, COLS:] = A[c, 2 * q, cols - COLS : cols, 0:rows]
-            return carry
-
-        lax.fori_loop(0, PML // 2, pack_aux_pair, 0)
-        each(x_aux + y_aux, "start")()
-
-    when(high_part, each(y_low, "start"))
-    each(y_high, "start")()
+    when(at_front, send_aux)
+    for k, (at, n) in enumerate(chunks):
+        if k == 0:
+            each(stage_low, "wait")()
+        if 2 * at == half:
+            when(at_back, send_aux)
+            each(stage_high, "wait")()
+        lax.fori_loop(at, at + n, pack_pair, 0)
+        each(x_halo[k], "start")()
+        if k == 0:
+            when(high_part, each(y_low, "start"))
+            each(y_high, "start")()
 
     def clear(lo, n):
         def plane(a, carry):
@@ -200,20 +207,6 @@
 
     clear(0, PAD)
     when(jnp.logical_and(at_back, high_part), lambda: clear(PAD + half, half))
-
-    each(x_low, "wait")()
-    when(has_pred, each(z_passed, "start"))
-    when(high_part, each(yx_low, "start"))
-    each(x_mat, "wait")()
-    each(yx_mat, "start")()
-
-    @pl.when(at_edge)
-    def _():
-        each(x_aux, "wait")()
-        each(yx_aux, "start")()
-
-    each(x_high, "wait")()
-    each(yx_high, "start")()
 
     def joined(r, l):
         low = lax.broadcasted_iota(jnp.int32, (2 * COLS, 2 * rows), 0) < COLS
@@ -256,9 +249,9 @@
             if not absorbing:
                 return g
             inside, at, b = rates[i]
-            s_new = b * states[i][c] + (b - 1.0) * g
-            new_states.append((c, at, s_new))
-            return jnp.where(inside, g + s_new, g)
+            g_new = jnp.where(inside, b * (g + states[i][c]), g)
+            new_states.append((c, at, g_new - g))
+            return g_new
 
         new_h = []
         for i in range(GROUP):
@@ -289,79 +282,149 @@
         for c, at, value in new_states:
             A[c, at] = value
 
-    def sweep(s, lo, n_groups, top):
+    def sweep(s, lo):
         shift = PAD + s + jnp.where(at_front, 0, planes - PML) - start
-
-        def body(g, carry):
-            a = PAD + lo + GROUP * g
-            inside = jnp.logical_and(at_edge, jnp.logical_and(a + GROUP > shift, a < shift + PML))
-            when(inside, lambda: group(a, s, shift, True))
-            when(jnp.logical_not(inside), lambda: group(a, s, shift, False))
-
-            if top is not None:
-                @pl.when(jnp.logical_and(at_back, high_part))
-                def _():
-                    def plane(p, carry):
-                        for c in range(3):
-                            F[c, p] = jnp.zeros((wide, 2 * rows), jnp.float32)
-                        return carry
-
-                    lax.fori_loop(jnp.maximum(a, PAD + top), a + GROUP, plane, 0)
-
-            return carry
-
-        lax.fori_loop(0, n_groups, body, 0)
-
-    each(load_high, "wait")()
-
-    @pl.when(low_part)
-    def _():
-        each(load_low, "wait")()
-        each(y_low + yx_low, "wait_recv")()
-
-    when(high_part, each(y_high + yx_high, "wait_recv"))
-    each(y_mat + yx_mat, "wait")()
-
-    @pl.when(at_edge)
-    def _():
+        a = PAD + lo
+        inside = jnp.logical_and(at_edge, jnp.logical_and(a + GROUP > shift, a < shift + PML))
+        when(inside, lambda: group(a, s, shift, True))
+        when(jnp.logical_not(inside), lambda: group(a, s, shift, False))
+
+        @pl.when(jnp.logical_and(at_back, high_part))
+        def _():
+            def plane(p, carry):
+                for c in range(3):
+                    F[c, p] = jnp.zeros((wide, 2 * rows), jnp.float32)
+                return carry
+
+            lax.fori_loop(jnp.maximum(a, PAD + half + s), a + GROUP, plane, 0)
+
+    def arrive(k):
+        each(x_halo[k], "wait")()
+        if k < half // SPAN:
+            when(has_pred, each(z_passed[k], "start"))
+            if k + 1 < half // SPAN:
+                when(has_pred, each(z_own[k + 1], "start"))
+            when(high_part, each(yx[k], "start"))
+        else:
+            each(yx[k], "start")()
+
+    def pass_aux():
+        each(x_aux, "wait")()
+        each(yx_aux, "start")()
+
+    def take_aux():
         each(y_aux + yx_aux, "wait")()
         lax.fori_loop(0, PML // 2, unpack_aux, 0)
 
-    lax.fori_loop(quads * gy, quads * gy + quads, unpack, 0)
+    n_half = half // SPAN
+    back_low = jnp.logical_and(at_back, low_part)
+    back_high = jnp.logical_and(at_back, high_part)
+
+    each(x_mat, "wait")()
+    each(yx_mat, "start")()
+    when(at_front, pass_aux)
+
+    @pl.when(high_part)
+    def _():
+        for k in range(n_half):
+            arrive(k)
+
+    when(back_high, pass_aux)
+    each(y_mat + yx_mat, "wait")()
     low = lax.broadcasted_iota(jnp.int32, (2 * COLS, 2 * rows), 0) < COLS
     mat[cols:wide] = jnp.where(low, halo_mat[0], halo_mat[1])
     core = mat[...] > 0.5
     eps_ref[...] = jnp.where(core, jnp.float32(eps_core), jnp.float32(eps_clad))
     kap_ref[...] = jnp.where(core, kerr_ref[1], kerr_ref[0])
 
-    def early(s, carry):
-        n_groups = (half - 1 - 2 * s + GROUP - 1) // GROUP
-        sweep(s, half - 1 - s - GROUP * n_groups, n_groups, None)
+    results = ((0, elec_out), (3, magn_out))
+    store, hand = [], []
+    for t in range(n_half):
+        there = [r.at[:, pl.ds(start + t * SPAN, SPAN)] for _, r in results]
+        store.append([local(fields(lo, STEPS + t * SPAN, SPAN, cols, own), r) for (lo, _), r in zip(results, there)])
+        hand.append([remote(fields(lo, STEPS + t * SPAN, SPAN, cols, far), r, other) for (lo, _), r in zip(results, there)])
+
+    def prepare(j):
+        @pl.when(low_part)
+        def _():
+            if j == 0:
+                each(load_low, "wait")()
+            if j == n_half:
+                each(load_high, "wait")()
+                when(at_back, pass_aux)
+            arrive(j)
+            if j == 0:
+                each(y_low, "wait_recv")()
+                when(at_front, take_aux)
+            if j == n_half:
+                each(y_high, "wait_recv")()
+                when(at_back, take_aux)
+            each(yx[j], "wait_recv")()
+
+        if j < n_half:
+            @pl.when(high_part)
+            def _():
+                if j == 0:
+                    each(load_high, "wait")()
+                arrive(j + n_half)
+                if j == 0:
+                    each(y_high, "wait_recv")()
+                    when(at_edge, take_aux)
+                each(yx[j + n_half], "wait_recv")()
+        else:
+            @pl.when(takes_z)
+            def _():
+                for sent, passed in z_from:
+                    each(sent[j - n_half] + passed[j - n_half], "wait_recv")()
+
+    def stage(j, carry):
+        for k in range(2 * n_half):
+            when(j == k, functools.partial(prepare, k))
+
+        @pl.when(jnp.logical_not(jnp.logical_and(back_high, j >= n_half)))
+        def _():
+            at = quads * gy + PAIRS * j
+            lax.fori_loop(at, at + PAIRS, unpack, 0)
+
+        def step(s, carry):
+            sweep(s, SPAN * j - 1 - s)
+            return carry
+
+        lax.fori_loop(0, jnp.where(j == 0, STEPS // 2, STEPS), step, 0)
+        for t in range(n_half):
+            when(j == t + n_half, each(hand[t] + store[t], "start"))
         return carry
 
-    lax.fori_loop(0, STEPS, early, 0)
-
-    when(low_part, each(y_high + yx_high, "wait_recv"))
-    when(takes_z, each(z_from, "wait_recv"))
-
-    @pl.when(jnp.logical_or(low_part, takes_z))
+    lax.fori_loop(0, 2 * n_half, stage, 0)
+
+    @pl.when(has_pred)
     def _():
-        lax.fori_loop(quads * gy + quads, quads * gy + 2 * quads, unpack, 0)
-
-    def late(s, carry):
-        sweep(s, half - 1 - s, half // GROUP, half + s)
-        return carry
-
-    lax.fori_loop(0, STEPS, late, 0)
-
-    results = ((0, elec_out), (3, magn_out))
-    store = [local(fields(lo, STEPS, half, cols, own), r.at[:, pl.ds(start, half)]) for lo, r in results]
-    hand = [remote(fields(lo, STEPS, half, cols, far), r.at[:, pl.ds(start, half)], other) for lo, r in results]
-    each(hand + store, "start")()
-    when(has_pred, each(z_own + z_passed, "wait_send"))
-    when(high_part, each(y_low + yx_low, "wait_send"))
-    each(y_high + yx_high, "wait_send")()
-    each(hand + store, "wait")()
+        for k in range(n_half):
+            each(z_own[k] + z_passed[k], "wait_send")()
+
+    @pl.when(high_part)
+    def _():
+        each(y_low, "wait_send")()
+        for k in range(n_half):
+            each(yx[k], "wait_send")()
+
+    each(y_high, "wait_send")()
+    for k in range(n_half, 2 * n_half):
+        each(yx[k], "wait_send")()
+    for t in range(n_half):
+        each(hand[t] + store[t], "wait")()
+
+
+def write_out(e_ref, h_ref, elec_out, magn_out, sem):
+    copies = [
+        pltpu.make_async_copy(src.at[c], dst.at[c], sem.at[i, c])
+        for i, (src, dst) in enumerate(((e_ref, elec_out), (h_ref, magn_out)))
+        for c in range(3)
+    ]
+    for copy in copies:
+        copy.start()
+    for copy in copies:
+        copy.wait()
 
 
 def shards(sizes, electric, magnetic, aux_state, material, kerr_strength):
@@ -369,11 +432,12 @@
     wide, deep = cols + 2 * COLS, planes + HALO
     f32 = jnp.float32
     any_space = pl.BlockSpec(memory_space=pl.ANY)
+    hbm = pl.BlockSpec(memory_space=pltpu.HBM)
     shape = jax.ShapeDtypeStruct(electric.shape, f32)
-    return pl.pallas_call(
+    fields = pl.pallas_call(
         functools.partial(kernel, sizes),
         out_shape=(shape, shape),
-        in_specs=[pl.BlockSpec(memory_space=pltpu.SMEM), any_space, any_space, any_space, any_space],
+        in_specs=[pl.BlockSpec(memory_space=pltpu.SMEM), hbm, hbm, hbm, hbm],
         out_specs=(any_space, any_space),
         scratch_shapes=[
             pltpu.VMEM((6, PAD + planes, wide, 2 * rows), f32),
@@ -389,16 +453,23 @@
             pltpu.VMEM((2, deep // 2, 6, 2 * COLS, 2 * rows), f32),
             pltpu.VMEM((2, PML // 2, 4, 2 * COLS, 2 * rows), f32),
             pltpu.VMEM((2, 2 * COLS, 2 * rows), f32),
-            pltpu.SemaphoreType.DMA((12,)),
-            pltpu.SemaphoreType.DMA((24,)),
-            pltpu.SemaphoreType.DMA((24,)),
-            pltpu.SemaphoreType.DMA((4,)),
-            pltpu.SemaphoreType.DMA((4, 2)),
+            pltpu.SemaphoreType.DMA((16,)),
+            pltpu.SemaphoreType.DMA((40,)),
+            pltpu.SemaphoreType.DMA((40,)),
+            pltpu.SemaphoreType.DMA((8,)),
+            pltpu.SemaphoreType.DMA((8, 2)),
         ],
         compiler_params=pltpu.CompilerParams(
             collective_id=0, has_side_effects=True, vmem_limit_bytes=60 * 2**20
         ),
     )(kerr_strength, electric, magnetic, aux_state, material)
+    return pl.pallas_call(
+        write_out,
+        out_shape=(shape, shape),
+        in_specs=[any_space, any_space],
+        out_specs=(hbm, hbm),
+        scratch_shapes=[pltpu.SemaphoreType.DMA((2, 3))],
+    )(*fields)
 
 
 def solution(mesh):

time: 28.8 us -> 50.5 us (1.75)
  Pallas kernels: 25.4 us -> 49.7 us
  local copies, waits for them, and re-layouts: 2.57 us -> 0 us
    pallas_call x0 -> x1, Pallas kernels: none -> 25 us  [shards(): pl.pallas_call(write_out, out_shape=(shape, shape), in_specs=[any_space,...]
    unnamed x4 -> x0, local copies, waits for them, and re-layouts: 2.57 us -> none
    pallas_call x1, Pallas kernels: 25.4 us -> 24.7 us  [shards(): pl.pallas_call(functools.partial(kernel, sizes), out_shape=(shape, shape)...]
where the time goes in v3:
time: 50.5 us; the launch traced here: 50.3 us
  Pallas kernels  49.7 us (98%)
  between operations  0.64 us (1%)
    pallas_call x1, Pallas kernels, shards(): pl.pallas_call(write_out, out_shape=(shape, shape), in_specs=[any_space,...  25 us
    pallas_call x1, Pallas kernels, shards(): pl.pallas_call(functools.partial(kernel, sizes), out_shape=(shape, shape)...  24.7 us

profile of v3, /device:TPU:0, one launch (start us, length us, event | category | flops | bytes accessed | tf_op | source)
XLA Modules:
  0.0 50.3 jit_solution(13953950646184348739)
XLA Ops:
  0.6 24.7 %shard_map.68 = (f32[3,16,16,128]{3,2,1,0:T(8,128)}, f32[3,16,16,128]{3,2,1,0:T(8,128)}) custom-call(f32[2]{0:T(128)} %kerr_ref.1, f32[3,16,16,128]{3,2,1,0:T(8,128)} %elec.1, f32[3,16,16,128]{3,2,1,0:T(8,128)} %magn.1, f32[4,2,8,16,128]{4,3,2,1,0:T(8,128)} %aux.1, s32[16,128]{1,0:T(8,128)} %material.1), custom_call_target="tpu_custom_call" | custom-call | tf_op jit(solution)/shard_map/pallas_call | solution.py:437
  25.3 25.0 %shard_map.69 = (f32[3,16,16,128]{3,2,1,0:T(8,128)}, f32[3,16,16,128]{3,2,1,0:T(8,128)}) custom-call(f32[3,16,16,128]{3,2,1,0:T(8,128)} %get-tuple-element.4.e_ref, f32[3,16,16,128]{3,2,1,0:T(8,128)} %get-tuple-element.5.h_ref), custom_call_target="tpu_custom_call" | custom-call | tf_op jit(solution)/shard_map/pallas_call | solution.py:466

commit v4 on v3

--- a/solution.py
+++ b/solution.py
@@ -102,7 +102,6 @@
     greet([left, right, other])()
     when(has_pred, greet([pred]))
     when(takes_z, greet(succ))
-    pl.semaphore_wait(barrier, 3 + has_pred.astype(jnp.int32) + 2 * takes_z.astype(jnp.int32))
 
     numbered = [0]
 
@@ -124,6 +123,9 @@
             device_id=pred, device_id_type=MESH,
         )
 
+    def staged(lo, at, n):
+        return own_fields.at[pl.ds(lo, 3), pl.ds(at, n)]
+
     def tiles(d, at, n, lanes):
         return halo.at[d, pl.ds(at, n), :, :, lanes]
 
@@ -132,10 +134,10 @@
     x_halo = [[remote(pack.at[d, pl.ds(at, n)], tiles(d, at, n, own), p) for d, p in both] for at, n in chunks]
     x_mat = [remote(pack_mat.at[d], halo_mat.at[d, :, own], p) for d, p in both]
     x_aux = [remote(pack_aux.at[d], halo_aux.at[d, :, :, :, own], p) for d, p in both]
-    y_low = [remote(r.at[:, pl.ds(0, half)], fields(lo, 0, half, cols, far), other) for lo, r in args]
-    y_high = [remote(r.at[:, pl.ds(half, half)], fields(lo, start, half, cols, far), other) for lo, r in args]
+    y_low = [remote(staged(lo, 0, half), fields(lo, 0, half, cols, far), other) for lo, r in args]
+    y_high = [remote(staged(lo, half, half), fields(lo, start, half, cols, far), other) for lo, r in args]
     yx = [[remote(tiles(d, at, n, own), tiles(d, at, n, far), other) for d in (0, 1)] for at, n in chunks]
-    y_aux = [remote(aux.at[:, side], A.at[:, pl.ds(0, PML), pl.ds(0, cols), far], other)]
+    y_aux = [remote(A.at[:, pl.ds(0, PML), pl.ds(0, cols), own], A.at[:, pl.ds(0, PML), pl.ds(0, cols), far], other)]
     yx_aux = [remote(halo_aux.at[d, :, :, :, own], halo_aux.at[d, :, :, :, far], other) for d in (0, 1)]
     y_mat = [remote(mat.at[pl.ds(0, cols), own], mat.at[pl.ds(0, cols), far], other)]
     yx_mat = [remote(halo_mat.at[d, :, own], halo_mat.at[d, :, far], other) for d in (0, 1)]
@@ -145,7 +147,7 @@
         sent, passed = [], []
         for k in range(half // SPAN):
             sent.append([
-                z_remote(r.at[:, pl.ds(k * SPAN, SPAN)], fields(lo, half + k * SPAN, SPAN, cols, lanes), sender)
+                z_remote(staged(lo, k * SPAN, SPAN), fields(lo, half + k * SPAN, SPAN, cols, lanes), sender)
                 for lo, r in args
             ])
             at, n = chunks[k]
@@ -154,8 +156,6 @@
 
     z_own, z_passed = z_copies(gy, z_lanes)
     z_from = [z_copies(0, far), z_copies(1, own)]
-
-    when(has_pred, each(z_own[0], "start"))
 
     def pack_pair(q, carry):
         for c in range(6):
@@ -173,25 +173,29 @@
             pack_aux[1, q, c, COLS:] = A[c, 2 * q, cols - COLS : cols, 0:rows]
         return carry
 
-    def send_aux():
-        load_aux.wait()
-        lax.fori_loop(0, PML // 2, pack_aux_pair, 0)
-        each(x_aux + y_aux, "start")()
-
     load_mat.wait()
     m = (mat_own[...] == 1).astype(jnp.float32)
     mat[0:cols, 0:rows] = m
     pack_mat[0] = m[0 : 2 * COLS]
     pack_mat[1] = m[cols - 2 * COLS : cols]
+    each(stage_low, "wait")()
+    lax.fori_loop(0, quads, pack_pair, 0)
+    each(stage_high, "wait")()
+    lax.fori_loop(quads, pairs, pack_pair, 0)
+
+    @pl.when(at_edge)
+    def _():
+        load_aux.wait()
+        lax.fori_loop(0, PML // 2, pack_aux_pair, 0)
+
+    pl.semaphore_wait(barrier, 3 + has_pred.astype(jnp.int32) + 2 * takes_z.astype(jnp.int32))
+
+    when(has_pred, each(z_own[0], "start"))
     each(x_mat + y_mat, "start")()
-    when(at_front, send_aux)
+    when(at_front, each(x_aux + y_aux, "start"))
     for k, (at, n) in enumerate(chunks):
-        if k == 0:
-            each(stage_low, "wait")()
         if 2 * at == half:
-            when(at_back, send_aux)
-            each(stage_high, "wait")()
-        lax.fori_loop(at, at + n, pack_pair, 0)
+            when(at_back, each(x_aux + y_aux, "start"))
         each(x_halo[k], "start")()
         if k == 0:
             when(high_part, each(y_low, "start"))
@@ -415,15 +419,17 @@
         each(hand[t] + store[t], "wait")()
 
 
-def write_out(e_ref, h_ref, elec_out, magn_out, sem):
-    copies = [
-        pltpu.make_async_copy(src.at[c], dst.at[c], sem.at[i, c])
-        for i, (src, dst) in enumerate(((e_ref, elec_out), (h_ref, magn_out)))
-        for c in range(3)
-    ]
-    for copy in copies:
+def write_out(e_ref, h_ref, elec_out, magn_out, held, in_sem, out_sem):
+    refs = ((e_ref, elec_out), (h_ref, magn_out))
+    parts = [(i, c) for i in range(2) for c in range(3)]
+    into = [pltpu.make_async_copy(refs[i][0].at[c], held.at[i, c], in_sem.at[i, c]) for i, c in parts]
+    back = [pltpu.make_async_copy(held.at[i, c], refs[i][1].at[c], out_sem.at[i, c]) for i, c in parts]
+    for copy in into:
         copy.start()
-    for copy in copies:
+    for first, second in zip(into, back):
+        first.wait()
+        second.start()
+    for copy in back:
         copy.wait()
 
 
@@ -468,7 +474,12 @@
         out_shape=(shape, shape),
         in_specs=[any_space, any_space],
         out_specs=(hbm, hbm),
-        scratch_shapes=[pltpu.SemaphoreType.DMA((2, 3))],
+        scratch_shapes=[
+            pltpu.VMEM((2,) + electric.shape, f32),
+            pltpu.SemaphoreType.DMA((2, 3)),
+            pltpu.SemaphoreType.DMA((2, 3)),
+        ],
+        compiler_params=pltpu.CompilerParams(vmem_limit_bytes=60 * 2**20),
     )(*fields)
 
 

time: 50.5 us -> 27.4 us (0.54)
  Pallas kernels: 49.7 us -> 26.6 us
    pallas_call x1, Pallas kernels: 25 us -> 1.97 us  [shards(): pl.pallas_call(write_out, out_shape=(shape, shape), in_specs=[any_space,...]
where the time goes in v4:
time: 27.4 us; the launch traced here: 27.2 us
  Pallas kernels  26.6 us (97%)
  between operations  0.64 us (2%)
    pallas_call x1, Pallas kernels, shards(): pl.pallas_call(functools.partial(kernel, sizes), out_shape=(shape, shape)...  24.6 us
    pallas_call x1, Pallas kernels, shards(): pl.pallas_call(write_out, out_shape=(shape, shape), in_specs=[any_space,...  1.97 us

profile of v4, /device:TPU:0, one launch (start us, length us, event | category | flops | bytes accessed | tf_op | source)
XLA Modules:
  0.0 27.2 jit_solution(1882858578609983661)
XLA Ops:
  0.6 24.6 %shard_map.68 = (f32[3,16,16,128]{3,2,1,0:T(8,128)}, f32[3,16,16,128]{3,2,1,0:T(8,128)}) custom-call(f32[2]{0:T(128)} %kerr_ref.1, f32[3,16,16,128]{3,2,1,0:T(8,128)} %elec.1, f32[3,16,16,128]{3,2,1,0:T(8,128)} %magn.1, f32[4,2,8,16,128]{4,3,2,1,0:T(8,128)} %aux.1, s32[16,128]{1,0:T(8,128)} %material.1), custom_call_target="tpu_custom_call" | custom-call | tf_op jit(solution)/shard_map/pallas_call | solution.py:443
  25.2 2.0 %shard_map.69 = (f32[3,16,16,128]{3,2,1,0:T(8,128)}, f32[3,16,16,128]{3,2,1,0:T(8,128)}) custom-call(f32[3,16,16,128]{3,2,1,0:T(8,128)} %get-tuple-element.4.e_ref, f32[3,16,16,128]{3,2,1,0:T(8,128)} %get-tuple-element.5.h_ref), custom_call_target="tpu_custom_call" | custom-call | tf_op jit(solution)/shard_map/pallas_call | solution.py:472

commit v5 on v4

--- a/solution.py
+++ b/solution.py
@@ -13,7 +13,8 @@
 HALO = 2 * STEPS
 COLS = STEPS
 PAD = 4
-GROUP = SPAN = 4
+GROUP = 2
+SPAN = 4
 PAIRS = SPAN // 2
 
 courant = 0.5
@@ -391,7 +392,8 @@
             lax.fori_loop(at, at + PAIRS, unpack, 0)
 
         def step(s, carry):
-            sweep(s, SPAN * j - 1 - s)
+            for i in range(SPAN // GROUP):
+                sweep(s, SPAN * j - 1 - s + GROUP * i)
             return carry
 
         lax.fori_loop(0, jnp.where(j == 0, STEPS // 2, STEPS), step, 0)

time: 27.4 us -> 29.2 us (1.066)
  Pallas kernels: 26.6 us -> 28.4 us
    pallas_call x1, Pallas kernels: 24.6 us -> 26.4 us  [shards(): pl.pallas_call(functools.partial(kernel, sizes), out_shape=(shape, shape)...]
where the time goes in v5:
time: 29.2 us; the launch traced here: 29 us
  Pallas kernels  28.4 us (97%)
  between operations  0.64 us (2%)
    pallas_call x1, Pallas kernels, shards(): pl.pallas_call(functools.partial(kernel, sizes), out_shape=(shape, shape)...  26.4 us
    pallas_call x1, Pallas kernels, shards(): pl.pallas_call(write_out, out_shape=(shape, shape), in_specs=[any_space,...  1.97 us

profile of v5, /device:TPU:0, one launch (start us, length us, event | category | flops | bytes accessed | tf_op | source)
XLA Modules:
  0.0 29.0 jit_solution(7960794888640060537)
XLA Ops:
  0.6 26.4 %shard_map.68 = (f32[3,16,16,128]{3,2,1,0:T(8,128)}, f32[3,16,16,128]{3,2,1,0:T(8,128)}) custom-call(f32[2]{0:T(128)} %kerr_ref.1, f32[3,16,16,128]{3,2,1,0:T(8,128)} %elec.1, f32[3,16,16,128]{3,2,1,0:T(8,128)} %magn.1, f32[4,2,8,16,128]{4,3,2,1,0:T(8,128)} %aux.1, s32[16,128]{1,0:T(8,128)} %material.1), custom_call_target="tpu_custom_call" | custom-call | tf_op jit(solution)/shard_map/pallas_call | solution.py:445
  27.1 2.0 %shard_map.69 = (f32[3,16,16,128]{3,2,1,0:T(8,128)}, f32[3,16,16,128]{3,2,1,0:T(8,128)}) custom-call(f32[3,16,16,128]{3,2,1,0:T(8,128)} %get-tuple-element.4.e_ref, f32[3,16,16,128]{3,2,1,0:T(8,128)} %get-tuple-element.5.h_ref), custom_call_target="tpu_custom_call" | custom-call | tf_op jit(solution)/shard_map/pallas_call | solution.py:474

commit v6 on v4

--- a/solution.py
+++ b/solution.py
@@ -15,6 +15,7 @@
 PAD = 4
 GROUP = SPAN = 4
 PAIRS = SPAN // 2
+AHEAD = 2
 
 courant = 0.5
 pml_rate = 3.0
@@ -193,13 +194,10 @@
     when(has_pred, each(z_own[0], "start"))
     each(x_mat + y_mat, "start")()
     when(at_front, each(x_aux + y_aux, "start"))
-    for k, (at, n) in enumerate(chunks):
-        if 2 * at == half:
-            when(at_back, each(x_aux + y_aux, "start"))
+    for k in range(AHEAD):
         each(x_halo[k], "start")()
-        if k == 0:
-            when(high_part, each(y_low, "start"))
-            each(y_high, "start")()
+    when(high_part, each(y_low, "start"))
+    each(y_high, "start")()
 
     def clear(lo, n):
         def plane(a, carry):
@@ -304,6 +302,10 @@
 
     def arrive(k):
         each(x_halo[k], "wait")()
+        if k == 0:
+            when(at_back, each(x_aux + y_aux, "start"))
+        if k + AHEAD < len(x_halo):
+            each(x_halo[k + AHEAD], "start")()
         if k < half // SPAN:
             when(has_pred, each(z_passed[k], "start"))
             if k + 1 < half // SPAN:

time: 27.4 us -> 27.3 us (level)
  no operation moved by 1% of the time
where the time goes in v6:
time: 27.3 us; the launch traced here: 27.1 us
  Pallas kernels  26.5 us (97%)
  between operations  0.64 us (2%)
    pallas_call x1, Pallas kernels, shards(): pl.pallas_call(functools.partial(kernel, sizes), out_shape=(shape, shape)...  24.5 us
    pallas_call x1, Pallas kernels, shards(): pl.pallas_call(write_out, out_shape=(shape, shape), in_specs=[any_space,...  1.97 us

profile of v6, /device:TPU:0, one launch (start us, length us, event | category | flops | bytes accessed | tf_op | source)
XLA Modules:
  0.0 27.1 jit_solution(8609501232729511764)
XLA Ops:
  0.6 24.5 %shard_map.68 = (f32[3,16,16,128]{3,2,1,0:T(8,128)}, f32[3,16,16,128]{3,2,1,0:T(8,128)}) custom-call(f32[2]{0:T(128)} %kerr_ref.1, f32[3,16,16,128]{3,2,1,0:T(8,128)} %elec.1, f32[3,16,16,128]{3,2,1,0:T(8,128)} %magn.1, f32[4,2,8,16,128]{4,3,2,1,0:T(8,128)} %aux.1, s32[16,128]{1,0:T(8,128)} %material.1), custom_call_target="tpu_custom_call" | custom-call | tf_op jit(solution)/shard_map/pallas_call | solution.py:445
  25.2 2.0 %shard_map.69 = (f32[3,16,16,128]{3,2,1,0:T(8,128)}, f32[3,16,16,128]{3,2,1,0:T(8,128)}) custom-call(f32[3,16,16,128]{3,2,1,0:T(8,128)} %get-tuple-element.4.e_ref, f32[3,16,16,128]{3,2,1,0:T(8,128)} %get-tuple-element.5.h_ref), custom_call_target="tpu_custom_call" | custom-call | tf_op jit(solution)/shard_map/pallas_call | solution.py:474

commit v7 on v6

--- a/solution.py
+++ b/solution.py
@@ -14,6 +14,7 @@
 COLS = STEPS
 PAD = 4
 GROUP = SPAN = 4
+STRIDE = 2
 PAIRS = SPAN // 2
 AHEAD = 2
 
@@ -56,6 +57,7 @@
     succ = [{"gz": jnp.minimum(gz + 1, n_gz - 1), "gy": part} for part in (0, 1)]
     own, far = pl.ds(0, rows), pl.ds(rows, rows)
     z_lanes = pl.ds(pl.multiple_of((1 - gy) * rows, rows), rows)
+    back_high = jnp.logical_and(at_back, high_part)
     start = half * gy
     side = jnp.where(at_front, 0, 1)
     args = ((0, elec), (3, magn))
@@ -208,6 +210,8 @@
         lax.fori_loop(lo, lo + n, plane, 0)
 
     clear(0, PAD)
+    for c in range(4):
+        A[c, PML] = jnp.zeros((wide, 2 * rows), jnp.float32)
     when(jnp.logical_and(at_back, high_part), lambda: clear(PAD + half, half))
 
     def joined(r, l):
@@ -227,78 +231,72 @@
 
     nx, ny = wide - 1, 2 * rows - 1
 
-    def group(a, s, shift, absorbing):
-        E = [[F[c, a + i] for c in range(3)] for i in range(GROUP + 1)]
-        H = [[F[c, a + i] for c in range(3, 6)] for i in range(GROUP)]
-        before = F[3, a - 1], F[4, a - 1]
-        rates = []
-        states = []
-        if absorbing:
-            for i in range(GROUP):
-                k = a + i - shift
-                inside = jnp.logical_and(k >= 0, k < PML)
-                at = jnp.where(inside, k, PML)
-                m = jnp.where(at_front, PML - 1 - k, k)
-                b = jnp.float32(DEPTH_RATES[0])
-                for j in range(1, PML):
-                    b = jnp.where(m == j, jnp.float32(DEPTH_RATES[j]), b)
-                rates.append((inside, at, b))
-                states.append([A[c, at] for c in range(4)])
-
-        new_states = []
-
-        def absorb(c, i, g):
-            if not absorbing:
-                return g
-            inside, at, b = rates[i]
-            g_new = jnp.where(inside, b * (g + states[i][c]), g)
-            new_states.append((c, at, g_new - g))
-            return g_new
-
-        new_h = []
-        for i in range(GROUP):
-            ex, ey, ez = E[i]
-            slope_y = absorb(0, i, E[i + 1][1] - ey)
-            slope_x = absorb(1, i, E[i + 1][0] - ex)
-            hx = H[i][0] - courant * ((pltpu.roll(ez, ny, 1) - ez) - slope_y)
-            hy = H[i][1] - courant * (slope_x - (pltpu.roll(ez, nx, 0) - ez))
-            hz = H[i][2] - courant * ((pltpu.roll(ey, nx, 0) - ey) - (pltpu.roll(ex, ny, 1) - ex))
-            new_h.append((hx, hy, hz))
-        new_e = []
-        for i in range(GROUP):
-            ex, ey, ez = E[i]
-            hx, hy, hz = new_h[i]
-            below = before if i == 0 else new_h[i - 1]
-            factor = courant / (eps_ref[...] + kap_ref[...] * (ex * ex + ey * ey + ez * ez))
-            slope_hy = absorb(2, i, hy - below[1])
-            slope_hx = absorb(3, i, hx - below[0])
-            new_e.append((
-                ex + factor * ((hz - pltpu.roll(hz, 1, 1)) - slope_hy),
-                ey + factor * (slope_hx - (hz - pltpu.roll(hz, 1, 0))),
-                ez + factor * ((hy - pltpu.roll(hy, 1, 0)) - (hx - pltpu.roll(hx, 1, 1))),
-            ))
-        for i in range(GROUP):
-            for c in range(3):
-                F[c, a + i] = new_e[i][c]
-                F[3 + c, a + i] = new_h[i][c]
-        for c, at, value in new_states:
-            A[c, at] = value
-
-    def sweep(s, lo):
-        shift = PAD + s + jnp.where(at_front, 0, planes - PML) - start
-        a = PAD + lo
-        inside = jnp.logical_and(at_edge, jnp.logical_and(a + GROUP > shift, a < shift + PML))
-        when(inside, lambda: group(a, s, shift, True))
-        when(jnp.logical_not(inside), lambda: group(a, s, shift, False))
-
-        @pl.when(jnp.logical_and(at_back, high_part))
-        def _():
-            def plane(p, carry):
-                for c in range(3):
-                    F[c, p] = jnp.zeros((wide, 2 * rows), jnp.float32)
-                return carry
-
-            lax.fori_loop(jnp.maximum(a, PAD + half + s), a + GROUP, plane, 0)
+    def steps(base, s, absorbing):
+        known = {}
+
+        def load(c, at):
+            return known[c, at] if (c, at) in known else F[c, base + at]
+
+        def advance(i):
+            low = -i
+            E = [[load(c, low + p) for c in range(3)] for p in range(GROUP + 1)]
+            H = [[load(c, low + p) for c in range(3, 6)] for p in range(GROUP)]
+            before = load(3, low - 1), load(4, low - 1)
+            rates = []
+            if absorbing:
+                shift = PAD + s + i + jnp.where(at_front, 0, planes - PML) - start
+                for p in range(GROUP):
+                    k = base + low + p - shift
+                    inside = jnp.logical_and(k >= 0, k < PML)
+                    m = jnp.where(at_front, PML - 1 - k, k)
+                    b = jnp.float32(1.0)
+                    for j in range(PML):
+                        b = jnp.where(m == j, jnp.float32(DEPTH_RATES[j]), b)
+                    beyond = jnp.logical_and(back_high, base + low + p >= PAD + half + s + i)
+                    rates.append((jnp.where(inside, k, PML), b, beyond))
+            new_states = []
+            states = [[A[c, at] for c in range(4)] for at, _, _ in rates]
+
+            def absorb(c, p, g):
+                if not absorbing:
+                    return g
+                at, b, _ = rates[p]
+                g_new = b * (g + states[p][c])
+                new_states.append((c, at, g_new - g))
+                return g_new
+
+            new_h, new_e = [], []
+            for p in range(GROUP):
+                ex, ey, ez = E[p]
+                slope_y = absorb(0, p, E[p + 1][1] - ey)
+                slope_x = absorb(1, p, E[p + 1][0] - ex)
+                hx = H[p][0] - courant * ((pltpu.roll(ez, ny, 1) - ez) - slope_y)
+                hy = H[p][1] - courant * (slope_x - (pltpu.roll(ez, nx, 0) - ez))
+                hz = H[p][2] - courant * ((pltpu.roll(ey, nx, 0) - ey) - (pltpu.roll(ex, ny, 1) - ex))
+                new_h.append((hx, hy, hz))
+            for p in range(GROUP):
+                ex, ey, ez = E[p]
+                hx, hy, hz = new_h[p]
+                below = before if p == 0 else new_h[p - 1]
+                factor = courant / (eps_ref[...] + kap_ref[...] * (ex * ex + ey * ey + ez * ez))
+                if absorbing:
+                    factor = jnp.where(rates[p][2], 0.0, factor)
+                slope_hy = absorb(2, p, hy - below[1])
+                slope_hx = absorb(3, p, hx - below[0])
+                new_e.append((
+                    ex + factor * ((hz - pltpu.roll(hz, 1, 1)) - slope_hy),
+                    ey + factor * (slope_hx - (hz - pltpu.roll(hz, 1, 0))),
+                    ez + factor * ((hy - pltpu.roll(hy, 1, 0)) - (hx - pltpu.roll(hx, 1, 1))),
+                ))
+            for p in range(GROUP):
+                for c, value in enumerate(new_e[p] + new_h[p]):
+                    known[c, low + p] = value
+                    F[c, base + low + p] = value
+            for c, at, value in new_states:
+                A[c, at] = value
+
+        for i in range(STRIDE):
+            advance(i)
 
     def arrive(k):
         each(x_halo[k], "wait")()
@@ -323,9 +321,6 @@
         lax.fori_loop(0, PML // 2, unpack_aux, 0)
 
     n_half = half // SPAN
-    back_low = jnp.logical_and(at_back, low_part)
-    back_high = jnp.logical_and(at_back, high_part)
-
     each(x_mat, "wait")()
     each(yx_mat, "start")()
     when(at_front, pass_aux)
@@ -392,11 +387,14 @@
             at = quads * gy + PAIRS * j
             lax.fori_loop(at, at + PAIRS, unpack, 0)
 
-        def step(s, carry):
-            sweep(s, SPAN * j - 1 - s)
+        def some_steps(r, carry):
+            s = STRIDE * r
+            base = PAD + SPAN * j - 1 - s
+            when(at_edge, lambda: steps(base, s, True))
+            when(jnp.logical_not(at_edge), lambda: steps(base, s, False))
             return carry
 
-        lax.fori_loop(0, jnp.where(j == 0, STEPS // 2, STEPS), step, 0)
+        lax.fori_loop(0, jnp.where(j == 0, STEPS // 2, STEPS) // STRIDE, some_steps, 0)
         for t in range(n_half):
             when(j == t + n_half, each(hand[t] + store[t], "start"))
         return carry

time: 27.3 us -> 27.4 us (level)
  no operation moved by 1% of the time
where the time goes in v7:
time: 27.4 us; the launch traced here: 27.2 us
  Pallas kernels  26.6 us (97%)
  between operations  0.64 us (2%)
    pallas_call x1, Pallas kernels, shards(): pl.pallas_call(functools.partial(kernel, sizes), out_shape=(shape, shape)...  24.6 us
    pallas_call x1, Pallas kernels, shards(): pl.pallas_call(write_out, out_shape=(shape, shape), in_specs=[any_space,...  1.97 us

profile of v7, /device:TPU:0, one launch (start us, length us, event | category | flops | bytes accessed | tf_op | source)
XLA Modules:
  0.0 27.2 jit_solution(17118770308075888474)
XLA Ops:
  0.6 24.6 %shard_map.68 = (f32[3,16,16,128]{3,2,1,0:T(8,128)}, f32[3,16,16,128]{3,2,1,0:T(8,128)}) custom-call(f32[2]{0:T(128)} %kerr_ref.1, f32[3,16,16,128]{3,2,1,0:T(8,128)} %elec.1, f32[3,16,16,128]{3,2,1,0:T(8,128)} %magn.1, f32[4,2,8,16,128]{4,3,2,1,0:T(8,128)} %aux.1, s32[16,128]{1,0:T(8,128)} %material.1), custom_call_target="tpu_custom_call" | custom-call | tf_op jit(solution)/shard_map/pallas_call | solution.py:443
  25.2 2.0 %shard_map.69 = (f32[3,16,16,128]{3,2,1,0:T(8,128)}, f32[3,16,16,128]{3,2,1,0:T(8,128)}) custom-call(f32[3,16,16,128]{3,2,1,0:T(8,128)} %get-tuple-element.4.e_ref, f32[3,16,16,128]{3,2,1,0:T(8,128)} %get-tuple-element.5.h_ref), custom_call_target="tpu_custom_call" | custom-call | tf_op jit(solution)/shard_map/pallas_call | solution.py:472

commit v8 on v7

--- a/solution.py
+++ b/solution.py
@@ -55,15 +55,14 @@
     other = {"gy": 1 - gy}
     pred = {"gz": jnp.maximum(gz - 1, 0), "gy": 1}
     succ = [{"gz": jnp.minimum(gz + 1, n_gz - 1), "gy": part} for part in (0, 1)]
-    own, far = pl.ds(0, rows), pl.ds(rows, rows)
-    z_lanes = pl.ds(pl.multiple_of((1 - gy) * rows, rows), rows)
+    own, far = 0, 1
     back_high = jnp.logical_and(at_back, high_part)
     start = half * gy
     side = jnp.where(at_front, 0, 1)
     args = ((0, elec), (3, magn))
 
-    def fields(lo, at, n, width, lanes):
-        return F.at[pl.ds(lo, 3), pl.ds(PAD + at, n), pl.ds(0, width), lanes]
+    def fields(lo, at, n, width, part):
+        return F.at[part, pl.ds(lo, 3), pl.ds(PAD + at, n), pl.ds(0, width)]
 
     def when(condition, work):
         pl.when(condition)(work)
@@ -84,7 +83,7 @@
     stage_low = [local(r.at[:, pl.ds(0, half)], own_fields.at[pl.ds(lo, 3), pl.ds(0, half)]) for lo, r in args]
     stage_high = [local(r.at[:, pl.ds(half, half)], own_fields.at[pl.ds(lo, 3), pl.ds(half, half)]) for lo, r in args]
     load_mat = local(material, mat_own)
-    load_aux = local(aux.at[:, side], A.at[:, pl.ds(0, PML), pl.ds(0, cols), own])
+    load_aux = local(aux.at[:, side], A.at[own, :, pl.ds(0, PML), pl.ds(0, cols)])
     load_low = [local(r.at[:, pl.ds(0, half)], fields(lo, 0, half, cols, own)) for lo, r in args]
     load_high = [local(r.at[:, pl.ds(half, half)], fields(lo, half - start, half, cols, own)) for lo, r in args]
     for copy in stage_low + stage_high + [load_mat]:
@@ -129,35 +128,35 @@
     def staged(lo, at, n):
         return own_fields.at[pl.ds(lo, 3), pl.ds(at, n)]
 
-    def tiles(d, at, n, lanes):
-        return halo.at[d, pl.ds(at, n), :, :, lanes]
+    def tiles(d, at, n, part):
+        return halo.at[part, d, pl.ds(at, n)]
 
     both = ((0, left), (1, right))
     chunks = [(k * PAIRS, PAIRS) for k in range(pairs // PAIRS)]
     x_halo = [[remote(pack.at[d, pl.ds(at, n)], tiles(d, at, n, own), p) for d, p in both] for at, n in chunks]
-    x_mat = [remote(pack_mat.at[d], halo_mat.at[d, :, own], p) for d, p in both]
-    x_aux = [remote(pack_aux.at[d], halo_aux.at[d, :, :, :, own], p) for d, p in both]
+    x_mat = [remote(pack_mat.at[d], halo_mat.at[own, d], p) for d, p in both]
+    x_aux = [remote(pack_aux.at[d], halo_aux.at[own, d], p) for d, p in both]
     y_low = [remote(staged(lo, 0, half), fields(lo, 0, half, cols, far), other) for lo, r in args]
     y_high = [remote(staged(lo, half, half), fields(lo, start, half, cols, far), other) for lo, r in args]
     yx = [[remote(tiles(d, at, n, own), tiles(d, at, n, far), other) for d in (0, 1)] for at, n in chunks]
-    y_aux = [remote(A.at[:, pl.ds(0, PML), pl.ds(0, cols), own], A.at[:, pl.ds(0, PML), pl.ds(0, cols), far], other)]
-    yx_aux = [remote(halo_aux.at[d, :, :, :, own], halo_aux.at[d, :, :, :, far], other) for d in (0, 1)]
-    y_mat = [remote(mat.at[pl.ds(0, cols), own], mat.at[pl.ds(0, cols), far], other)]
-    yx_mat = [remote(halo_mat.at[d, :, own], halo_mat.at[d, :, far], other) for d in (0, 1)]
-
-    def z_copies(sender, lanes):
+    y_aux = [remote(A.at[own, :, pl.ds(0, PML), pl.ds(0, cols)], A.at[far, :, pl.ds(0, PML), pl.ds(0, cols)], other)]
+    yx_aux = [remote(halo_aux.at[own, d], halo_aux.at[far, d], other) for d in (0, 1)]
+    y_mat = [remote(mat.at[own, pl.ds(0, cols)], mat.at[far, pl.ds(0, cols)], other)]
+    yx_mat = [remote(halo_mat.at[own, d], halo_mat.at[far, d], other) for d in (0, 1)]
+
+    def z_copies(sender, part):
         z_numbered[0] = 0
         sent, passed = [], []
         for k in range(half // SPAN):
             sent.append([
-                z_remote(staged(lo, k * SPAN, SPAN), fields(lo, half + k * SPAN, SPAN, cols, lanes), sender)
+                z_remote(staged(lo, k * SPAN, SPAN), fields(lo, half + k * SPAN, SPAN, cols, part), sender)
                 for lo, r in args
             ])
             at, n = chunks[k]
-            passed.append([z_remote(tiles(d, at, n, own), tiles(d, pairs + at, n, lanes), sender) for d in (0, 1)])
+            passed.append([z_remote(tiles(d, at, n, own), tiles(d, pairs + at, n, part), sender) for d in (0, 1)])
         return sent, passed
 
-    z_own, z_passed = z_copies(gy, z_lanes)
+    z_own, z_passed = z_copies(gy, 1 - gy)
     z_from = [z_copies(0, far), z_copies(1, own)]
 
     def pack_pair(q, carry):
@@ -170,15 +169,15 @@
 
     def pack_aux_pair(q, carry):
         for c in range(4):
-            pack_aux[0, q, c, 0:COLS] = A[c, 2 * q, 0:COLS, 0:rows]
-            pack_aux[0, q, c, COLS:] = A[c, 2 * q + 1, 0:COLS, 0:rows]
-            pack_aux[1, q, c, 0:COLS] = A[c, 2 * q + 1, cols - COLS : cols, 0:rows]
-            pack_aux[1, q, c, COLS:] = A[c, 2 * q, cols - COLS : cols, 0:rows]
+            pack_aux[0, q, c, 0:COLS] = A[0, c, 2 * q, 0:COLS]
+            pack_aux[0, q, c, COLS:] = A[0, c, 2 * q + 1, 0:COLS]
+            pack_aux[1, q, c, 0:COLS] = A[0, c, 2 * q + 1, cols - COLS : cols]
+            pack_aux[1, q, c, COLS:] = A[0, c, 2 * q, cols - COLS : cols]
         return carry
 
     load_mat.wait()
     m = (mat_own[...] == 1).astype(jnp.float32)
-    mat[0:cols, 0:rows] = m
+    mat[0, 0:cols] = m
     pack_mat[0] = m[0 : 2 * COLS]
     pack_mat[1] = m[cols - 2 * COLS : cols]
     each(stage_low, "wait")()
@@ -203,39 +202,52 @@
 
     def clear(lo, n):
         def plane(a, carry):
-            for c in range(6):
-                F[c, a] = jnp.zeros((wide, 2 * rows), jnp.float32)
+            for h in range(2):
+                for c in range(6):
+                    F[h, c, a] = jnp.zeros((wide, rows), jnp.float32)
             return carry
 
         lax.fori_loop(lo, lo + n, plane, 0)
 
     clear(0, PAD)
-    for c in range(4):
-        A[c, PML] = jnp.zeros((wide, 2 * rows), jnp.float32)
+    for h in range(2):
+        for c in range(4):
+            A[h, c, PML] = jnp.zeros((wide, rows), jnp.float32)
     when(jnp.logical_and(at_back, high_part), lambda: clear(PAD + half, half))
 
     def joined(r, l):
-        low = lax.broadcasted_iota(jnp.int32, (2 * COLS, 2 * rows), 0) < COLS
+        low = lax.broadcasted_iota(jnp.int32, (2 * COLS, rows), 0) < COLS
         return jnp.where(low, r, l), pltpu.roll(jnp.where(low, l, r), COLS, 0)
 
     def unpack(q, carry):
         at = PAD + 2 * q - start
-        for c in range(6):
-            F[c, at, cols:wide], F[c, at + 1, cols:wide] = joined(halo[0, q, c], halo[1, q, c])
+        for h in range(2):
+            for c in range(6):
+                F[h, c, at, cols:wide], F[h, c, at + 1, cols:wide] = joined(halo[h, 0, q, c], halo[h, 1, q, c])
         return carry
 
     def unpack_aux(q, carry):
-        for c in range(4):
-            A[c, 2 * q, cols:wide], A[c, 2 * q + 1, cols:wide] = joined(halo_aux[0, q, c], halo_aux[1, q, c])
+        for h in range(2):
+            for c in range(4):
+                A[h, c, 2 * q, cols:wide], A[h, c, 2 * q + 1, cols:wide] = joined(
+                    halo_aux[h, 0, q, c], halo_aux[h, 1, q, c]
+                )
         return carry
 
     nx, ny = wide - 1, 2 * rows - 1
+
+    def whole(ref, c, at):
+        return jnp.concatenate([ref[0, c, at], ref[1, c, at]], 1)
+
+    def put(ref, c, at, value):
+        ref[0, c, at] = value[:, 0:rows]
+        ref[1, c, at] = value[:, rows:]
 
     def steps(base, s, absorbing):
         known = {}
 
         def load(c, at):
-            return known[c, at] if (c, at) in known else F[c, base + at]
+            return known[c, at] if (c, at) in known else whole(F, c, base + at)
 
         def advance(i):
             low = -i
@@ -255,7 +267,7 @@
                     beyond = jnp.logical_and(back_high, base + low + p >= PAD + half + s + i)
                     rates.append((jnp.where(inside, k, PML), b, beyond))
             new_states = []
-            states = [[A[c, at] for c in range(4)] for at, _, _ in rates]
+            states = [[whole(A, c, at) for c in range(4)] for at, _, _ in rates]
 
             def absorb(c, p, g):
                 if not absorbing:
@@ -291,9 +303,9 @@
             for p in range(GROUP):
                 for c, value in enumerate(new_e[p] + new_h[p]):
                     known[c, low + p] = value
-                    F[c, base + low + p] = value
+                    put(F, c, base + low + p, value)
             for c, at, value in new_states:
-                A[c, at] = value
+                put(A, c, at, value)
 
         for i in range(STRIDE):
             advance(i)
@@ -332,9 +344,10 @@
 
     when(back_high, pass_aux)
     each(y_mat + yx_mat, "wait")()
-    low = lax.broadcasted_iota(jnp.int32, (2 * COLS, 2 * rows), 0) < COLS
-    mat[cols:wide] = jnp.where(low, halo_mat[0], halo_mat[1])
-    core = mat[...] > 0.5
+    low = lax.broadcasted_iota(jnp.int32, (2 * COLS, rows), 0) < COLS
+    for h in range(2):
+        mat[h, cols:wide] = jnp.where(low, halo_mat[h, 0], halo_mat[h, 1])
+    core = jnp.concatenate([mat[0], mat[1]], 1) > 0.5
     eps_ref[...] = jnp.where(core, jnp.float32(eps_core), jnp.float32(eps_clad))
     kap_ref[...] = jnp.where(core, kerr_ref[1], kerr_ref[0])
 
@@ -446,19 +459,19 @@
         in_specs=[pl.BlockSpec(memory_space=pltpu.SMEM), hbm, hbm, hbm, hbm],
         out_specs=(any_space, any_space),
         scratch_shapes=[
-            pltpu.VMEM((6, PAD + planes, wide, 2 * rows), f32),
-            pltpu.VMEM((4, PML + 1, wide, 2 * rows), f32),
+            pltpu.VMEM((2, 6, PAD + planes, wide, rows), f32),
+            pltpu.VMEM((2, 4, PML + 1, wide, rows), f32),
             pltpu.VMEM((wide, 2 * rows), f32),
             pltpu.VMEM((wide, 2 * rows), f32),
-            pltpu.VMEM((wide, 2 * rows), f32),
+            pltpu.VMEM((2, wide, rows), f32),
             pltpu.VMEM((cols, rows), jnp.int32),
             pltpu.VMEM((6, planes, cols, rows), f32),
             pltpu.VMEM((2, planes // 2, 6, 2 * COLS, rows), f32),
             pltpu.VMEM((2, PML // 2, 4, 2 * COLS, rows), f32),
             pltpu.VMEM((2, 2 * COLS, rows), f32),
-            pltpu.VMEM((2, deep // 2, 6, 2 * COLS, 2 * rows), f32),
-            pltpu.VMEM((2, PML // 2, 4, 2 * COLS, 2 * rows), f32),
-            pltpu.VMEM((2, 2 * COLS, 2 * rows), f32),
+            pltpu.VMEM((2, 2, deep // 2, 6, 2 * COLS, rows), f32),
+            pltpu.VMEM((2, 2, PML // 2, 4, 2 * COLS, rows), f32),
+            pltpu.VMEM((2, 2, 2 * COLS, rows), f32),
             pltpu.SemaphoreType.DMA((16,)),
             pltpu.SemaphoreType.DMA((40,)),
             pltpu.SemaphoreType.DMA((40,)),

time: 27.4 us -> 27.5 us (level)
  no operation moved by 1% of the time
where the time goes in v8:
time: 27.5 us; the launch traced here: 27.3 us
  Pallas kernels  26.7 us (97%)
  between operations  0.64 us (2%)
    pallas_call x1, Pallas kernels, shards(): pl.pallas_call(functools.partial(kernel, sizes), out_shape=(shape, shape)...  24.7 us
    pallas_call x1, Pallas kernels, shards(): pl.pallas_call(write_out, out_shape=(shape, shape), in_specs=[any_space,...  1.97 us

profile of v8, /device:TPU:0, one launch (start us, length us, event | category | flops | bytes accessed | tf_op | source)
XLA Modules:
  0.0 27.3 jit_solution(7639765684398178644)
XLA Ops:
  0.6 24.7 %shard_map.68 = (f32[3,16,16,128]{3,2,1,0:T(8,128)}, f32[3,16,16,128]{3,2,1,0:T(8,128)}) custom-call(f32[2]{0:T(128)} %kerr_ref.1, f32[3,16,16,128]{3,2,1,0:T(8,128)} %elec.1, f32[3,16,16,128]{3,2,1,0:T(8,128)} %magn.1, f32[4,2,8,16,128]{4,3,2,1,0:T(8,128)} %aux.1, s32[16,128]{1,0:T(8,128)} %material.1), custom_call_target="tpu_custom_call" | custom-call | tf_op jit(solution)/shard_map/pallas_call | solution.py:456
  25.3 2.0 %shard_map.69 = (f32[3,16,16,128]{3,2,1,0:T(8,128)}, f32[3,16,16,128]{3,2,1,0:T(8,128)}) custom-call(f32[3,16,16,128]{3,2,1,0:T(8,128)} %get-tuple-element.4.e_ref, f32[3,16,16,128]{3,2,1,0:T(8,128)} %get-tuple-element.5.h_ref), custom_call_target="tpu_custom_call" | custom-call | tf_op jit(solution)/shard_map/pallas_call | solution.py:485

commit v9 on v8

--- a/solution.py
+++ b/solution.py
@@ -12,6 +12,7 @@
 STEPS = 4
 HALO = 2 * STEPS
 COLS = STEPS
+LEAD = 8
 PAD = 4
 GROUP = SPAN = 4
 STRIDE = 2
@@ -62,7 +63,7 @@
     args = ((0, elec), (3, magn))
 
     def fields(lo, at, n, width, part):
-        return F.at[part, pl.ds(lo, 3), pl.ds(PAD + at, n), pl.ds(0, width)]
+        return F.at[part, pl.ds(lo, 3), pl.ds(PAD + at, n), pl.ds(LEAD, width)]
 
     def when(condition, work):
         pl.when(condition)(work)
@@ -204,7 +205,7 @@
         def plane(a, carry):
             for h in range(2):
                 for c in range(6):
-                    F[h, c, a] = jnp.zeros((wide, rows), jnp.float32)
+                    F[h, c, a] = jnp.zeros((LEAD + wide + LEAD, rows), jnp.float32)
             return carry
 
         lax.fori_loop(lo, lo + n, plane, 0)
@@ -223,7 +224,11 @@
         at = PAD + 2 * q - start
         for h in range(2):
             for c in range(6):
-                F[h, c, at, cols:wide], F[h, c, at + 1, cols:wide] = joined(halo[h, 0, q, c], halo[h, 1, q, c])
+                halves = joined(halo[h, 0, q, c], halo[h, 1, q, c])
+                for i in range(2):
+                    F[h, c, at + i, LEAD + cols : LEAD + wide] = halves[i]
+                    if c in (1, 2):
+                        F[h, c, at + i, LEAD + wide : LEAD + wide + 1] = F[h, c, at + i, LEAD : LEAD + 1]
         return carry
 
     def unpack_aux(q, carry):
@@ -234,7 +239,7 @@
                 )
         return carry
 
-    nx, ny = wide - 1, 2 * rows - 1
+    ny = 2 * rows - 1
 
     def whole(ref, c, at):
         return jnp.concatenate([ref[0, c, at], ref[1, c, at]], 1)
@@ -243,17 +248,31 @@
         ref[0, c, at] = value[:, 0:rows]
         ref[1, c, at] = value[:, rows:]
 
+    def plane_of(c, at, by=0):
+        first = LEAD + by
+        return jnp.concatenate([F[h, c, at, first : first + wide] for h in range(2)], 1)
+
+    def put_plane(c, at, value):
+        for h in range(2):
+            part = value[:, h * rows : (h + 1) * rows]
+            F[h, c, at, LEAD : LEAD + wide] = part
+            if c in (1, 2):
+                F[h, c, at, LEAD + wide : LEAD + wide + 1] = part[0:1]
+            if c in (4, 5):
+                F[h, c, at, LEAD - 1 : LEAD] = part[wide - 1 : wide]
+
     def steps(base, s, absorbing):
         known = {}
 
         def load(c, at):
-            return known[c, at] if (c, at) in known else whole(F, c, base + at)
+            return known[c, at] if (c, at) in known else plane_of(c, base + at)
 
         def advance(i):
             low = -i
             E = [[load(c, low + p) for c in range(3)] for p in range(GROUP + 1)]
             H = [[load(c, low + p) for c in range(3, 6)] for p in range(GROUP)]
             before = load(3, low - 1), load(4, low - 1)
+            ahead = [[plane_of(c, base + low + p, 1) for c in (1, 2)] for p in range(GROUP)]
             rates = []
             if absorbing:
                 shift = PAD + s + i + jnp.where(at_front, 0, planes - PML) - start
@@ -283,13 +302,16 @@
                 slope_y = absorb(0, p, E[p + 1][1] - ey)
                 slope_x = absorb(1, p, E[p + 1][0] - ex)
                 hx = H[p][0] - courant * ((pltpu.roll(ez, ny, 1) - ez) - slope_y)
-                hy = H[p][1] - courant * (slope_x - (pltpu.roll(ez, nx, 0) - ez))
-                hz = H[p][2] - courant * ((pltpu.roll(ey, nx, 0) - ey) - (pltpu.roll(ex, ny, 1) - ex))
+                hy = H[p][1] - courant * (slope_x - (ahead[p][1] - ez))
+                hz = H[p][2] - courant * ((ahead[p][0] - ey) - (pltpu.roll(ex, ny, 1) - ex))
                 new_h.append((hx, hy, hz))
+                for c in range(3):
+                    put_plane(3 + c, base + low + p, new_h[p][c])
             for p in range(GROUP):
                 ex, ey, ez = E[p]
                 hx, hy, hz = new_h[p]
                 below = before if p == 0 else new_h[p - 1]
+                hy_b, hz_b = plane_of(4, base + low + p, -1), plane_of(5, base + low + p, -1)
                 factor = courant / (eps_ref[...] + kap_ref[...] * (ex * ex + ey * ey + ez * ez))
                 if absorbing:
                     factor = jnp.where(rates[p][2], 0.0, factor)
@@ -297,13 +319,14 @@
                 slope_hx = absorb(3, p, hx - below[0])
                 new_e.append((
                     ex + factor * ((hz - pltpu.roll(hz, 1, 1)) - slope_hy),
-                    ey + factor * (slope_hx - (hz - pltpu.roll(hz, 1, 0))),
-                    ez + factor * ((hy - pltpu.roll(hy, 1, 0)) - (hx - pltpu.roll(hx, 1, 1))),
+                    ey + factor * (slope_hx - (hz - hz_b)),
+                    ez + factor * ((hy - hy_b) - (hx - pltpu.roll(hx, 1, 1))),
                 ))
             for p in range(GROUP):
                 for c, value in enumerate(new_e[p] + new_h[p]):
                     known[c, low + p] = value
-                    put(F, c, base + low + p, value)
+                    if c < 3:
+                        put_plane(c, base + low + p, value)
             for c, at, value in new_states:
                 put(A, c, at, value)
 
@@ -459,7 +482,7 @@
         in_specs=[pl.BlockSpec(memory_space=pltpu.SMEM), hbm, hbm, hbm, hbm],
         out_specs=(any_space, any_space),
         scratch_shapes=[
-            pltpu.VMEM((2, 6, PAD + planes, wide, rows), f32),
+            pltpu.VMEM((2, 6, PAD + planes, LEAD + wide + LEAD, rows), f32),
             pltpu.VMEM((2, 4, PML + 1, wide, rows), f32),
             pltpu.VMEM((wide, 2 * rows), f32),
             pltpu.VMEM((wide, 2 * rows), f32),

time: 27.5 us -> 27.6 us (level)
  no operation moved by 1% of the time
where the time goes in v9:
time: 27.6 us; the launch traced here: 27.4 us
  Pallas kernels  26.8 us (97%)
  between operations  0.64 us (2%)
    pallas_call x1, Pallas kernels, shards(): pl.pallas_call(functools.partial(kernel, sizes), out_shape=(shape, shape)...  24.8 us
    pallas_call x1, Pallas kernels, shards(): pl.pallas_call(write_out, out_shape=(shape, shape), in_specs=[any_space,...  1.97 us

profile of v9, /device:TPU:0, one launch (start us, length us, event | category | flops | bytes accessed | tf_op | source)
XLA Modules:
  0.0 27.4 jit_solution(4678593040432100013)
XLA Ops:
  0.6 24.8 %shard_map.68 = (f32[3,16,16,128]{3,2,1,0:T(8,128)}, f32[3,16,16,128]{3,2,1,0:T(8,128)}) custom-call(f32[2]{0:T(128)} %kerr_ref.1, f32[3,16,16,128]{3,2,1,0:T(8,128)} %elec.1, f32[3,16,16,128]{3,2,1,0:T(8,128)} %magn.1, f32[4,2,8,16,128]{4,3,2,1,0:T(8,128)} %aux.1, s32[16,128]{1,0:T(8,128)} %material.1), custom_call_target="tpu_custom_call" | custom-call | tf_op jit(solution)/shard_map/pallas_call | solution.py:479
  25.4 2.0 %shard_map.69 = (f32[3,16,16,128]{3,2,1,0:T(8,128)}, f32[3,16,16,128]{3,2,1,0:T(8,128)}) custom-call(f32[3,16,16,128]{3,2,1,0:T(8,128)} %get-tuple-element.4.e_ref, f32[3,16,16,128]{3,2,1,0:T(8,128)} %get-tuple-element.5.h_ref), custom_call_target="tpu_custom_call" | custom-call | tf_op jit(solution)/shard_map/pallas_call | solution.py:508

commit v10 on v6

--- a/solution.py
+++ b/solution.py
@@ -32,7 +32,7 @@
     sizes,
     kerr_ref, elec, magn, aux, material,
     elec_out, magn_out,
-    F, A, eps_ref, kap_ref, mat, mat_own, own_fields,
+    F, A, eps_ref, kap_ref, mat, mat_own, own_fields, handed,
     pack, pack_aux, pack_mat,
     halo, halo_aux, halo_mat,
     local_sem, send_sem, recv_sem, z_send_sem, z_recv_sem,
@@ -344,11 +344,14 @@
     kap_ref[...] = jnp.where(core, kerr_ref[1], kerr_ref[0])
 
     results = ((0, elec_out), (3, magn_out))
-    store, hand = [], []
+    store, hand, store_handed = [], [], []
     for t in range(n_half):
         there = [r.at[:, pl.ds(start + t * SPAN, SPAN)] for _, r in results]
         store.append([local(fields(lo, STEPS + t * SPAN, SPAN, cols, own), r) for (lo, _), r in zip(results, there)])
-        hand.append([remote(fields(lo, STEPS + t * SPAN, SPAN, cols, far), r, other) for (lo, _), r in zip(results, there)])
+        landed = [handed.at[pl.ds(lo, 3), pl.ds(t * SPAN, SPAN)] for lo, _ in results]
+        hand.append([remote(fields(lo, STEPS + t * SPAN, SPAN, cols, far), r, other) for (lo, _), r in zip(results, landed)])
+        theirs = [r.at[:, pl.ds(half - start + t * SPAN, SPAN)] for _, r in results]
+        store_handed.append([local(src, r) for src, r in zip(landed, theirs)])
 
     def prepare(j):
         @pl.when(low_part)
@@ -418,7 +421,12 @@
     for k in range(n_half, 2 * n_half):
         each(yx[k], "wait_send")()
     for t in range(n_half):
-        each(hand[t] + store[t], "wait")()
+        for copy, on in zip(hand[t], store_handed[t]):
+            copy.wait_recv()
+            on.start()
+    for t in range(n_half):
+        each(hand[t], "wait_send")()
+        each(store[t] + store_handed[t], "wait")()
 
 
 def write_out(e_ref, h_ref, elec_out, magn_out, held, in_sem, out_sem):
@@ -455,13 +463,14 @@
             pltpu.VMEM((wide, 2 * rows), f32),
             pltpu.VMEM((cols, rows), jnp.int32),
             pltpu.VMEM((6, planes, cols, rows), f32),
+            pltpu.VMEM((6, planes // 2, cols, rows), f32),
             pltpu.VMEM((2, planes // 2, 6, 2 * COLS, rows), f32),
             pltpu.VMEM((2, PML // 2, 4, 2 * COLS, rows), f32),
             pltpu.VMEM((2, 2 * COLS, rows), f32),
             pltpu.VMEM((2, deep // 2, 6, 2 * COLS, 2 * rows), f32),
             pltpu.VMEM((2, PML // 2, 4, 2 * COLS, 2 * rows), f32),
             pltpu.VMEM((2, 2 * COLS, 2 * rows), f32),
-            pltpu.SemaphoreType.DMA((16,)),
+            pltpu.SemaphoreType.DMA((24,)),
             pltpu.SemaphoreType.DMA((40,)),
             pltpu.SemaphoreType.DMA((40,)),
             pltpu.SemaphoreType.DMA((8,)),

time: 27.3 us -> 27.9 us (1.022)
  Pallas kernels: 26.5 us -> 27.1 us
    pallas_call x1, Pallas kernels: 24.5 us -> 25.1 us  [shards(): pl.pallas_call(functools.partial(kernel, sizes), out_shape=(shape, shape)...]
where the time goes in v10:
time: 27.9 us; the launch traced here: 27.7 us
  Pallas kernels  27.1 us (97%)
  between operations  0.64 us (2%)
    pallas_call x1, Pallas kernels, shards(): pl.pallas_call(functools.partial(kernel, sizes), out_shape=(shape, shape)...  25.1 us
    pallas_call x1, Pallas kernels, shards(): pl.pallas_call(write_out, out_shape=(shape, shape), in_specs=[any_space,...  1.97 us

profile of v10, /device:TPU:0, one launch (start us, length us, event | category | flops | bytes accessed | tf_op | source)
XLA Modules:
  0.0 27.7 jit_solution(17380521549572992367)
XLA Ops:
  0.6 25.1 %shard_map.68 = (f32[3,16,16,128]{3,2,1,0:T(8,128)}, f32[3,16,16,128]{3,2,1,0:T(8,128)}) custom-call(f32[2]{0:T(128)} %kerr_ref.1, f32[3,16,16,128]{3,2,1,0:T(8,128)} %elec.1, f32[3,16,16,128]{3,2,1,0:T(8,128)} %magn.1, f32[4,2,8,16,128]{4,3,2,1,0:T(8,128)} %aux.1, s32[16,128]{1,0:T(8,128)} %material.1), custom_call_target="tpu_custom_call" | custom-call | tf_op jit(solution)/shard_map/pallas_call | solution.py:453
  25.7 2.0 %shard_map.69 = (f32[3,16,16,128]{3,2,1,0:T(8,128)}, f32[3,16,16,128]{3,2,1,0:T(8,128)}) custom-call(f32[3,16,16,128]{3,2,1,0:T(8,128)} %get-tuple-element.4.e_ref, f32[3,16,16,128]{3,2,1,0:T(8,128)} %get-tuple-element.5.h_ref), custom_call_target="tpu_custom_call" | custom-call | tf_op jit(solution)/shard_map/pallas_call | solution.py:483
